TPU v7x, 32 devices: a whole 2x2x4 slice. The times are simulated.
32 devices in a mesh: row: 8 (over z, y), col: 4 (over x, core).
Axes of the slice: x: 2, y: 2, z: 4, core: 2. Of those that a mesh axis runs over, the one named last changes fastest.
Arguments:
- rhs: float32 [32, 65536], P(None, ('row', 'col')), may hold values from -5 to 7
- coords: float32 [3, 65536], P(None, ('row', 'col')), may hold values from 0 to 8, as said below
- nugget: float32 [65536], P(('row', 'col')), may hold values from 1.5 to 3
- near_ids: int32 [128, 3], P(('row', 'col')), may hold values from -1 to 127, as said below
- basis: float32 [7, 128, 65536], P(None, None, ('row', 'col')), may hold values from -6 to 6
Outputs:
- solution: float32 [32, 65536], P(None, ('row', 'col'))
- residual: float32 [32, 65536], P(None, ('row', 'col'))
Inputs may be any that keep to these rules, and one draw needn't show every extreme that they name: `near_ids`: row i lists leaf i and some of the leaves i - 1 to i + 1 inside the range, each at most once, in any order; the other slots hold -1; the first and last leaf of each device's block of 4 list all such leaves inside the range. `coords`: each leaf's points lie in a unit box with an integer corner; consecutive leaves lie in boxes that share a face.
All inputs are finite; a program needn't handle non-finite values.
Results may differ from a plain program's by a relative error of at most 0.0003.
Values sent between devices are 32-bit elements; how exact they have to be, the bound alone decides.
No kernel may reach another device: no remote copies, remote signals or barrier semaphores. Data moves between devices by JAX's collectives and lax.ppermute only.
A program may use at most 128 MiB of HBM per device.

v0:
```python
import functools

import jax
import jax.numpy as jnp
from jax import lax
from jax.experimental import pallas as pl
from jax.experimental.pallas import tpu as pltpu
from jax.sharding import PartitionSpec as P

LEAF = 512
ITERS = 4
WIN = 3
LANES = 128
LOCAL = 3
CHUNK = 16
NORM_TILE = 8
PRODUCTS_TILE = 16
FLOPS = 3 * 10**9

root_three = 1.7320508075688772
spacing_factor = 1.6
matern_scale = root_three / (spacing_factor * LEAF ** (-1.0 / 3.0))

BOTH = ("row", "col")
ROWS_COLS = (((1,), (0,)), ((), ()))
ROWS_ROWS = (((1,), (1,)), ((), ()))

PAIRS = ("dq", "rq", "qq", "rw", "qw", "dw", "rz", "qz", "dz")


def halves(values):
    high = values.astype(jnp.bfloat16)
    low = (values - high.astype(jnp.float32)).astype(jnp.bfloat16)
    return high, low


def stacked(values):
    return jnp.concatenate(halves(values), axis=0)


def product(stack, high, low, dims):
    rows = stack.shape[0] // 2
    main = lax.dot_general(stack, high, dims, preferred_element_type=jnp.float32)
    rest = lax.dot_general(stack[:rows], low, dims, preferred_element_type=jnp.float32)
    return main[:rows] + (main[rows:] + rest)


def row_sum(values):
    return jnp.sum(values, axis=1, keepdims=True)


def in_lanes(columns, shape):
    lane = lax.broadcasted_iota(jnp.int32, shape, 1)
    block = jnp.zeros(shape, jnp.float32)
    for index, column in enumerate(columns):
        block = jnp.where(lane == index, column, block)
    return block


def sums_tile(columns, rows, depth):
    turned = in_lanes(columns, (rows, LANES)).T[:depth]
    return jnp.concatenate([turned, jnp.zeros((depth, LANES - rows), jnp.float32)], axis=1)


def level_terms(core, columns, rows, depth):
    twice = [jnp.concatenate([column, column], axis=0) for column in columns]
    zero = jnp.zeros((rows, 1), jnp.float32)
    tile = sums_tile([zero] * (len(PAIRS) - len(columns)) + twice, rows, depth)
    lane = lax.broadcasted_iota(jnp.int32, tile.shape, 1)
    return jnp.where(lane // (rows // 2) == core, tile, 0.0)


def chosen(core, odd, even):
    return jnp.where(core == 1, odd, even)


def whole(memory=pltpu.VMEM):
    return pl.BlockSpec(memory_space=memory)


def call(body, outs, *args, scalars=0, flops=0, limit=32):
    return pl.pallas_call(
        body,
        out_shape=outs,
        in_specs=[whole(pltpu.SMEM)] * scalars + [whole()] * (len(args) - scalars),
        out_specs=[whole()] * len(outs),
        compiler_params=pltpu.CompilerParams(vmem_limit_bytes=limit * 2**20),
        cost_estimate=pl.CostEstimate(flops=flops, bytes_accessed=2**20, transcendentals=0),
    )(*args)


def f32(*shape):
    return jax.ShapeDtypeStruct(shape, jnp.float32)


def bf16(*shape):
    return jax.ShapeDtypeStruct(shape, jnp.bfloat16)


def matrix_rows(rows, lanes):
    square = None
    for axis in range(3):
        spread = rows[:, axis : axis + 1] - lanes[axis : axis + 1]
        square = spread * spread if square is None else square + spread * spread
    square = square * (matern_scale * matern_scale)
    scaled = square * lax.rsqrt(jnp.maximum(square, 1e-30))
    return halves((1.0 + scaled) * jnp.exp(-scaled))


def fill_matrices(pairs, lane_ref, sub_ref, high_ref, low_ref):
    for matrix, (row_leaf, col_leaf) in enumerate(pairs):
        lanes = lane_ref[:, col_leaf * LEAF : (col_leaf + 1) * LEAF]

        def one(part, carry):
            row_at = pl.multiple_of(row_leaf * LEAF + part * CHUNK, CHUNK)
            out_at = pl.ds(pl.multiple_of(part * CHUNK, CHUNK), CHUNK)
            values = matrix_rows(sub_ref[pl.ds(row_at, CHUNK)], lanes)
            high_ref[matrix, out_at], low_ref[matrix, out_at] = values
            return carry

        lax.fori_loop(0, LEAF // CHUNK, one, 0, unroll=4)


def setup_kernel(pairs, lane_ref, sub_ref, basis_ref, high_ref, low_ref, basis_high_ref, basis_low_ref, raw_ref, sem_ref):
    levels, rank, _ = basis_ref.shape
    copies = [pltpu.make_async_copy(basis_ref.at[at], raw_ref.at[at], sem_ref.at[at]) for at in range(levels)]
    for copy in copies:
        copy.start()
    fill_matrices(pairs, lane_ref, sub_ref, high_ref, low_ref)
    for at, copy in enumerate(copies):
        copy.wait()
        here = slice(at * rank, (at + 1) * rank)
        basis_high_ref[here], basis_low_ref[here] = halves(raw_ref[at])


def edge_matrices(core_ref, rows, sub_ref, paired_ref, other_ref, high_ref, low_ref):
    core = core_ref[0]
    leaves = sub_ref.shape[0] // LEAF
    here = slice(rows, rows + 3)
    lanes = [
        chosen(core, paired_ref[here], other_ref[here]),
        chosen(core, other_ref[here], paired_ref[here]),
    ]

    for side in range(2):
        first_row = side * (leaves - 1) * LEAF

        def one(part, carry):
            row_at = pl.multiple_of(first_row + part * CHUNK, CHUNK)
            out_at = pl.ds(pl.multiple_of(part * CHUNK, CHUNK), CHUNK)
            values = matrix_rows(sub_ref[pl.ds(row_at, CHUNK)], lanes[side])
            high_ref[side, out_at], low_ref[side, out_at] = values
            return carry

        lax.fori_loop(0, LEAF // CHUNK, one, 0, unroll=4)


def edges_kernel(core_ref, field_ref, coords_ref, paired_ref, other_ref):
    core = core_ref[0]
    rows, width = field_ref.shape
    pad = jnp.zeros((8 - 3, LEAF), jnp.float32)
    head = jnp.concatenate([field_ref[:, :LEAF], coords_ref[:, :LEAF], pad], axis=0)
    tail = jnp.concatenate([field_ref[:, width - LEAF :], coords_ref[:, width - LEAF :], pad], axis=0)
    paired_ref[...] = chosen(core, head, tail)
    other_ref[...] = chosen(core, tail, head)


def down_kernel(core_ref, field_ref, high_ref, low_ref, local_ref, keep_ref, send_ref, tile_ref):
    core = core_ref[0]
    rank = LANES
    rows, width = field_ref.shape
    half = width // 2
    stack = stacked(field_ref[...])
    for part in range(2):
        points = slice(part * half, (part + 1) * half)
        local_ref[:, part * rank : (part + 1) * rank] = product(
            stack[:, points], high_ref[:rank, points], low_ref[:rank, points], ROWS_ROWS
        )
    all_points = product(stack, high_ref[rank:], low_ref[rank:], ROWS_ROWS)
    local_ref[:, 2 * rank :] = all_points[:, :rank]
    own = rows // 2
    for bit in range(all_points.shape[1] // rank - 1):
        block = all_points[:, (bit + 1) * rank : (bit + 2) * rank]
        keep_ref[bit * own : (bit + 1) * own] = chosen(core, block[own:], block[:own])
        send_ref[bit * own : (bit + 1) * own] = chosen(core, block[:own], block[own:])
    tile_ref[...] = sums_tile([row_sum(field_ref[...] * field_ref[...])], rows, NORM_TILE)


def leaf_of(ref, leaf):
    return ref[:, leaf * LEAF : (leaf + 1) * LEAF]


def weight_of(place_ref, ids_ref, leaf, offset):
    target = place_ref[0] * ids_ref.shape[0] + leaf + offset
    found = ids_ref[leaf, 0] == target
    for slot in range(1, WIN):
        found = jnp.logical_or(found, ids_ref[leaf, slot] == target)
    return jnp.where(jnp.logical_and(found, target >= 0), 1.0 / (16 * WIN), 0.0)


def inner_kernel(half, place_ref, ids_ref, field_ref, nugget_ref, high_ref, low_ref, pair_high_ref, pair_low_ref, out_ref):
    leaves = ids_ref.shape[0]
    start = half * (leaves // 2)
    stop = start + leaves // 2
    pieces = {leaf: stacked(leaf_of(field_ref, leaf)) for leaf in range(max(start - 1, 0), min(stop + 1, leaves))}
    for leaf in range(start, stop):
        at = leaf - start
        inside = product(pieces[leaf], high_ref[at], low_ref[at], ROWS_COLS)
        total = leaf_of(nugget_ref, leaf) * leaf_of(field_ref, leaf) + weight_of(place_ref, ids_ref, leaf, 0) * inside
        if leaf > 0:
            before = product(pieces[leaf - 1], pair_high_ref[leaf - 1], pair_low_ref[leaf - 1], ROWS_COLS)
            total = total + weight_of(place_ref, ids_ref, leaf, -1) * before
        if leaf < leaves - 1:
            after = product(pieces[leaf + 1], pair_high_ref[leaf], pair_low_ref[leaf], ROWS_ROWS)
            total = total + weight_of(place_ref, ids_ref, leaf, 1) * after
        out_ref[:, at * LEAF : (at + 1) * LEAF] = total


def edge_kernel(sums, *refs):
    place_ref, core_ref, ids_ref, paired_ref, other_ref, high_ref, low_ref, front_ref, back_ref = refs[:9]
    refs = refs[9:]
    out_ref = refs[-2] if sums else refs[-1]
    core = core_ref[0]
    leaves = ids_ref.shape[0]
    rows, width = out_ref.shape
    before = chosen(core, paired_ref[:rows], other_ref[:rows])
    after = chosen(core, other_ref[:rows], paired_ref[:rows])
    out_ref[:, : width // 2] = front_ref[...]
    out_ref[:, width // 2 :] = back_ref[...]
    part = product(stacked(before), high_ref[0], low_ref[0], ROWS_ROWS)
    out_ref[:, :LEAF] += weight_of(place_ref, ids_ref, 0, -1) * part
    part = product(stacked(after), high_ref[1], low_ref[1], ROWS_ROWS)
    out_ref[:, width - LEAF :] += weight_of(place_ref, ids_ref, leaves - 1, 1) * part
    if not sums:
        return
    fields = dict(zip("rqdw", refs[:4]))
    locals_ = dict(zip("rqd", refs[4:7]))
    tile_ref = refs[-1]
    totals = {pair: jnp.zeros((rows, 1), jnp.float32) for pair in PAIRS}
    for leaf in range(leaves):
        here = {name: leaf_of(ref, leaf) for name, ref in fields.items()}
        here["z"] = leaf_of(out_ref, leaf)
        for left, right in PAIRS:
            totals[left + right] = totals[left + right] + row_sum(here[left] * here[right])
    for block in range(LOCAL):
        scale = 1.0 / (LEAF * (2 if block < 2 else 4))
        lanes = slice(block * LANES, (block + 1) * LANES)
        for name in "rqd":
            term = row_sum(locals_[name][:, lanes] * locals_["q"][:, lanes])
            totals[name + "z"] = totals[name + "z"] + scale * term
    tile_ref[...] = sums_tile([totals[pair] for pair in PAIRS], rows, PRODUCTS_TILE)


def combine_kernel(products, bit, cluster, *refs):
    refs = list(refs)
    core_ref, mine_ref, other_ref = refs[:3]
    refs = refs[3:]
    tile_ref = refs.pop(0) if bit == 0 else None
    if products:
        field_ref, direction_ref = refs[:2]
        refs = refs[2:]
    *level_refs, next_ref, level_ref = refs
    own = level_ref.shape[0]
    depth = PRODUCTS_TILE if products else NORM_TILE
    total = mine_ref[...] + other_ref[...]
    if bit == 0:
        tile = tile_ref[...]
    else:
        tile = total[total.shape[0] - depth :]
        total = total[: total.shape[0] - depth]
    level = total[:own]
    level_ref[...] = level
    if products:
        here = slice(bit * own, (bit + 1) * own)
        partners = [field_ref[here], level, direction_ref[here]]
        columns = [row_sum(level * partner) * (1.0 / cluster) for partner in partners]
        tile = tile + level_terms(core_ref[0], columns, 2 * own, depth)
    left = total.shape[0] - own
    if left:
        next_ref[:left] = total[own:]
        next_ref[left:] = tile
    else:
        for index, ref in enumerate(level_refs):
            next_ref[index * own : (index + 1) * own] = ref[...]
        next_ref[bit * own : (bit + 1) * own] = level
        next_ref[(bit + 1) * own :] = tile


def up_parts(core, mine_ref, other_ref, local_ref, rows, width, depth):
    own = rows // 2
    crossing = (mine_ref.shape[0] - depth) // own
    sums = (mine_ref[crossing * own :] + other_ref[crossing * own :]).T[:rows]
    scaled = []
    for bit in range(crossing):
        here = slice(bit * own, (bit + 1) * own)
        low_rows = chosen(core, other_ref[here], mine_ref[here])
        high_rows = chosen(core, mine_ref[here], other_ref[here])
        scaled.append(jnp.concatenate([low_rows, high_rows], axis=0) * (1.0 / (width * (2 << bit))))
    one = [local_ref[:, part * LANES : (part + 1) * LANES] * (1.0 / (2 * LEAF)) for part in range(2)]
    two = local_ref[:, 2 * LANES :] * (1.0 / (4 * LEAF))
    return sums, [stacked(jnp.concatenate([one[part], two] + scaled, axis=1)) for part in range(2)]


def own_rows(core, column, crossing):
    own = column.shape[0] // 2
    return jnp.concatenate([chosen(core, column[own:], column[:own])] * crossing, axis=0)


def put_edges(core, field_ref, paired_ref, send_ref):
    width = field_ref.shape[1]
    head = field_ref[:, :LEAF]
    tail = field_ref[:, width - LEAF :]
    paired_ref[...] = chosen(core, head, tail)
    send_ref[...] = chosen(core, tail, head)


def residual_up_kernel(first, *refs):
    core_ref, high_ref, low_ref, near_ref, mine_ref, other_ref, local_ref = refs[:7]
    refs = refs[7:]
    if first:
        image_ref, state_ref, paired_ref, send_ref = refs
        q_ref = image_ref
    else:
        field_ref, old_d_ref, old_q_ref, old_skel_ref, old_local_ref, old_state_ref = refs[:6]
        image_ref, state_ref, paired_ref, send_ref, d_ref, q_ref, skel_ref, new_local_ref = refs[6:]
    core = core_ref[0]
    rows, width = near_ref.shape
    half = width // 2
    sums, stacks = up_parts(core, mine_ref, other_ref, local_ref, rows, width, NORM_TILE)
    norm = sums[:, 0:1]
    state_ref[...] = in_lanes([norm], (rows, LANES))
    ratio = None if first else norm / old_state_ref[:, 0:1]
    for part in range(2):
        points = slice(part * half, (part + 1) * half)
        image = near_ref[:, points] + product(stacks[part], high_ref[:, points], low_ref[:, points], ROWS_COLS)
        image_ref[:, points] = image
        if not first:
            d_ref[:, points] = field_ref[:, points] + ratio * old_d_ref[:, points]
            q_ref[:, points] = image + ratio * old_q_ref[:, points]
    put_edges(core, q_ref, paired_ref, send_ref)
    if not first:
        rows_in = skel_ref.shape[0]
        crossing = rows_in // (rows // 2)
        skel_ref[...] = mine_ref[:rows_in] + own_rows(core, ratio, crossing) * old_skel_ref[...]
        new_local_ref[...] = local_ref[...] + ratio * old_local_ref[...]


def image_up_kernel(first, last, *refs):
    core_ref, high_ref, low_ref, near_ref, mine_ref, other_ref, local_ref = refs[:7]
    r_ref, w_ref, d_ref, q_ref, state_ref = refs[7:12]
    refs = refs[12:]
    if not first:
        solution_ref = refs[0]
        refs = refs[1:]
    if not last:
        r_skel_ref, d_skel_ref, r_local_ref, d_local_ref = refs[:4]
        refs = refs[4:]
    new_solution_ref, new_r_ref = refs[:2]
    if not last:
        new_d_ref, new_q_ref, new_skel_ref, new_local_ref, new_state_ref, paired_ref, send_ref = refs[2:]
    core = core_ref[0]
    rows, width = near_ref.shape
    half = width // 2
    sums, stacks = up_parts(core, mine_ref, other_ref, local_ref, rows, width, PRODUCTS_TILE)
    dot = {pair: sums[:, index : index + 1] for index, pair in enumerate(PAIRS)}
    norm = state_ref[:, 0:1]
    step = norm / dot["dq"]
    new_norm = norm - step * (2.0 * dot["rq"] - step * dot["qq"])
    ratio = new_norm / norm
    curve = dot["rw"] - step * (dot["qw"] + dot["rz"] - step * dot["qz"])
    curve = curve + ratio * (dot["dw"] - step * dot["dz"] + dot["rq"] - step * dot["qq"] + ratio * dot["dq"])
    new_step = new_norm / curve
    for part in range(2):
        points = slice(part * half, (part + 1) * half)
        image = near_ref[:, points] + product(stacks[part], high_ref[:, points], low_ref[:, points], ROWS_COLS)
        d = d_ref[:, points]
        q = q_ref[:, points]
        r = r_ref[:, points] - step * q
        new_q = w_ref[:, points] - step * image + ratio * q
        new_d = r + ratio * d
        moved = step * d + new_step * new_d
        new_solution_ref[:, points] = moved if first else solution_ref[:, points] + moved
        new_r_ref[:, points] = r - new_step * new_q
        if not last:
            new_d_ref[:, points] = new_d
            new_q_ref[:, points] = new_q
    if not last:
        rows_in = new_skel_ref.shape[0]
        crossing = rows_in // (rows // 2)
        r_skel = r_skel_ref[:rows_in] - own_rows(core, step, crossing) * mine_ref[:rows_in]
        new_skel_ref[...] = r_skel + own_rows(core, ratio, crossing) * d_skel_ref[:rows_in]
        new_local_ref[...] = r_local_ref[...] - step * local_ref[...] + ratio * d_local_ref[...]
        new_state_ref[...] = in_lanes([new_norm], (rows, LANES))
        put_edges(core, new_r_ref, paired_ref, send_ref)


def per_device(rhs, coords, nugget, near_ids, basis):
    rows, width = rhs.shape
    levels = basis.shape[0]
    leaves = width // LEAF
    own = rows // 2
    crossing = levels - (leaves.bit_length() - 1)
    devices = lax.axis_size("row") * lax.axis_size("col")
    place = jnp.reshape(lax.axis_index(BOTH), (1,))
    core = place % 2
    nugget = nugget[None, :]

    def swap(value, bit):
        return lax.ppermute(value, BOTH, [(source, source ^ (1 << bit)) for source in range(devices)])

    def halo(paired, other):
        outward = [(index, index + 1) for index in range(1, devices - 1, 2)]
        ends = [(0, 0), (devices - 1, devices - 1)]
        return swap(paired, 0), lax.ppermute(other, BOTH, outward + [(target, source) for source, target in outward] + ends)

    def down(field):
        shapes = [f32(rows, LOCAL * LANES)] + [f32(crossing * own, LANES)] * 2 + [f32(NORM_TILE, LANES)]
        return call(down_kernel, shapes, core, field, high, low, scalars=1, flops=FLOPS)

    def inner(half, field):
        args = [place, near_ids, field, nugget, *diagonal[half], *beside]
        body = functools.partial(inner_kernel, half)
        return call(body, [f32(rows, width // 2)], *args, scalars=2, flops=FLOPS // 2)[0]

    def edge(edges, front, back, *more):
        shapes = [f32(rows, width)] + ([f32(PRODUCTS_TILE, LANES)] if more else [])
        args = [place, core, near_ids, *edges, *outside, front, back, *more]
        return call(functools.partial(edge_kernel, bool(more)), shapes, *args, scalars=3, flops=FLOPS // 3)

    def chain(products, keep, got, tile, beside_steps, *skeletons):
        depth = PRODUCTS_TILE if products else NORM_TILE
        done = []
        results = []
        message = keep
        for bit in range(crossing):
            left = crossing - bit - 1
            args = [core, message, got] + ([tile] if bit == 0 else []) + list(skeletons) + (done if left == 0 else [])
            message, level = call(
                functools.partial(combine_kernel, products, bit, width * (2 << bit)),
                [f32((left or crossing) * own + depth, LANES), f32(own, LANES)],
                *args,
                scalars=1,
            )
            done.append(level)
            got = swap(message, bit + 1 if left else 0)
            if bit < len(beside_steps):
                got, result = lax.optimization_barrier((got, beside_steps[bit](message)))
                results.append(result)
        return message, got, results

    edges = halo(*call(edges_kernel, [f32(rows + 8, LEAF)] * 2, core, rhs, coords, scalars=1))
    turned = coords.T
    half = leaves // 2
    pairs = [(leaf, leaf) for leaf in range(half)]
    *front_diagonal, high, low = pl.pallas_call(
        functools.partial(setup_kernel, pairs),
        out_shape=[bf16(half, LEAF, LEAF)] * 2 + [bf16(levels * LANES, width)] * 2,
        in_specs=[whole(), whole(), whole(pltpu.HBM)],
        out_specs=[whole()] * 4,
        scratch_shapes=[pltpu.VMEM(basis.shape, jnp.float32), pltpu.SemaphoreType.DMA((levels,))],
        compiler_params=pltpu.CompilerParams(vmem_limit_bytes=46 * 2**20),
        cost_estimate=pl.CostEstimate(flops=FLOPS, bytes_accessed=2**20, transcendentals=0),
    )(coords, turned, basis)
    diagonal = [front_diagonal, None]
    beside = outside = None

    def after(message, *values):
        return lax.optimization_barrier((message, *values))[1:]

    def late_matrices(pairs):
        def run(message):
            shapes = [bf16(len(pairs), LEAF, LEAF)] * 2
            return call(functools.partial(fill_matrices, pairs), shapes, *after(message, coords, turned), flops=FLOPS)

        return run

    def late_edge_matrices(message):
        def body(core_ref, *refs):
            edge_matrices(core_ref, rows, *refs)

        args = after(message, turned, *edges)
        return call(body, [bf16(2, LEAF, LEAF)] * 2, core, *args, scalars=1, flops=FLOPS)

    solution, r, carried = None, rhs, None
    for step in range(0, ITERS, 2):
        first, last = step == 0, step + 2 == ITERS
        r_local, keep, part, tile = down(r)
        got = swap(part, 0)
        if first:
            work = [
                late_matrices([(leaf, leaf) for leaf in range(half, leaves)]),
                late_matrices([(leaf, leaf + 1) for leaf in range(leaves - 1)]),
                late_edge_matrices,
            ]
            message, got, results = chain(False, keep, got, tile, work)
            diagonal[1], beside, outside = results
            (near,) = edge(edges, inner(0, r), inner(1, r))
        else:
            fronts = []

            def front_work(message):
                fronts.append(inner(0, *after(message, r)))
                return fronts[0]

            def back_work(message):
                fronts.append(inner(1, *after(message, r)))
                return fronts[1]

            def edge_work(message):
                return edge(edges, *after(message, *fronts))[0]

            message, got, results = chain(False, keep, got, tile, [front_work, back_work, edge_work])
            near = results[2]
        args = [core, high, low, near, message, got, r_local]
        outs = [f32(rows, width), f32(rows, LANES)] + [f32(rows, LEAF)] * 2
        if first:
            w, state, *edges = call(
                functools.partial(residual_up_kernel, True), outs, *args, scalars=1, flops=FLOPS // 2
            )
            d, q, d_skel, d_local = r, w, message, r_local
        else:
            outs = outs + [f32(rows, width)] * 2 + [f32(crossing * own, LANES), f32(rows, LOCAL * LANES)]
            w, state, *edges, d, q, d_skel, d_local = call(
                functools.partial(residual_up_kernel, False), outs, *args, r, *carried, scalars=1, flops=FLOPS // 2
            )
        r_skel = message
        edges = halo(*edges)
        q_local, keep, part, _ = down(q)
        got = swap(part, 0)
        near, tile = edge(edges, inner(0, q), inner(1, q), r, q, d, w, r_local, q_local, d_local)
        message, got, _ = chain(True, keep, got, tile, [], r_skel, d_skel)
        args = [core, high, low, near, message, got, q_local, r, w, d, q, state]
        args = args + ([] if first else [solution]) + ([] if last else [r_skel, d_skel, r_local, d_local])
        outs = [f32(rows, width)] * 2
        if not last:
            outs = outs + [f32(rows, width)] * 2 + [f32(crossing * own, LANES), f32(rows, LOCAL * LANES)]
            outs = outs + [f32(rows, LANES)] + [f32(rows, LEAF)] * 2
        solution, r, *rest = call(
            functools.partial(image_up_kernel, first, last), outs, *args, scalars=1, flops=FLOPS // 2
        )
        if not last:
            carried = rest[:5]
            edges = halo(*rest[5:])
    return (solution, r)


def solution(mesh):
    placed = (
        P(None, BOTH),
        P(None, BOTH),
        P(BOTH),
        P(BOTH, None),
        P(None, None, BOTH),
    )
    return jax.shard_map(
        per_device,
        mesh=mesh,
        in_specs=placed,
        out_specs=(P(None, BOTH), P(None, BOTH)),
        check_vma=False,
    )
```

profile of v0, /device:TPU:0, one launch (start us, length us, event | category | flops | bytes accessed | tf_op | source)
XLA Modules:
  0.0 136.7 jit_solution(12066740237663628682)
XLA Ops:
  2.5 5.5 %shard_map.68 = (bf16[2,512,512]{2,1,0:T(8,128)(2,1)S(1)}, bf16[2,512,512]{2,1,0:T(8,128)(2,1)S(1)}, bf16[896,2048]{1,0:T(8,128)(2,1)S(1)}, bf16[896,2048]{1,0:T(8,128)(2,1)}) custom-call(f32[3,2048]{1,0:T(4,128)S(1)} %copy-done.5, f32[2048,3]{1,0:T(8,128)S(1)} %bitcast.3, f32[7,128,2048]{2,1,0:T(8,128)} %basis_ref.1), custom_call_target="tpu_custom_call" | custom-call | flops 3000000000 | bytes 1048576 | tf_op jit(solution)/shard_map/pallas_call | solution.py:455
  10.1 2.3 %shard_map.70 = (f32[32,384]{1,0:T(8,128)S(1)}, f32[80,128]{1,0:T(8,128)S(1)}, f32[80,128]{1,0:T(8,128)S(1)}, f32[8,128]{1,0:T(8,128)S(1)}) custom-call(s32[1]{0:T(128)S(6)} %select_n.7.core_ref.refs_0_.refs_1_, f32[32,2048]{1,0:T(8,128)S(1)} %copy-done.2, bf16[896,2048]{1,0:T(8,128)(2,1)S(1)} %get-tuple-element.113.high_ref.refs_1_, ...), custom_call_target="tpu_custom_call" | custom-call | flops 3000000000 | bytes 1048576 | tf_op jit(solution)/shard_map/pallas_call | solution.py:82
  13.8 4.2 %collective-permute-start.3 = (f32[72,128]{1,0:T(8,128)S(1)}, f32[72,128]{1,0:T(8,128)S(1)}, u32[]{:S(2)}, u32[]{:S(2)}) collective-permute-start(f32[72,128]{1,0:T(8,128)S(1)} %get-tuple-element.120.refs_1_), channel_id=1, source_target_pairs={{0,2},{1,3},{2,0},{3,1},{4,6},{5,7},{6,4},{7,5},{8,10},{9,11},{10,... | collective-permute-start | bytes 110600 | tf_op jit(solution)/shard_map/ppermute | solution.py:409
  18.0 2.7 %shard_map.72 = (bf16[2,512,512]{2,1,0:T(8,128)(2,1)S(1)}, bf16[2,512,512]{2,1,0:T(8,128)(2,1)S(1)}) custom-call(f32[3,2048]{1,0:T(4,128)S(1)} %copy-done.5, f32[2048,3]{1,0:T(8,128)S(1)} %bitcast.4), custom_call_target="tpu_custom_call" | custom-call | flops 3000000000 | bytes 1048576 | tf_op jit(solution)/shard_map/pallas_call | solution.py:82
  23.1 4.0 %shard_map.74 = (bf16[3,512,512]{2,1,0:T(8,128)(2,1)S(1)}, bf16[3,512,512]{2,1,0:T(8,128)(2,1)S(1)}) custom-call(f32[3,2048]{1,0:T(4,128)S(1)} %copy-done.5, f32[2048,3]{1,0:T(8,128)S(1)} %bitcast.5), custom_call_target="tpu_custom_call" | custom-call | flops 3000000000 | bytes 1048576 | tf_op jit(solution)/shard_map/pallas_call | solution.py:82
  27.2 2.2 %collective-permute-start.5 = (f32[40,128]{1,0:T(8,128)S(1)}, f32[40,128]{1,0:T(8,128)S(1)}, u32[]{:S(2)}, u32[]{:S(2)}) collective-permute-start(f32[40,128]{1,0:T(8,128)S(1)} %get-tuple-element.132.refs_1_), channel_id=1, source_target_pairs={{0,8},{1,9},{2,10},{3,11},{4,12},{5,13},{6,14},{7,15},{8,0},{9,1},... | collective-permute-start | bytes 61448 | tf_op jit(solution)/shard_map/ppermute | solution.py:409
  29.4 2.7 %shard_map.76 = (bf16[2,512,512]{2,1,0:T(8,128)(2,1)S(1)}, bf16[2,512,512]{2,1,0:T(8,128)(2,1)S(1)}) custom-call(s32[1]{0:T(128)S(6)} %select_n.7.core_ref.refs_0_.refs_1_, f32[2048,3]{1,0:T(8,128)S(1)} %bitcast.6, f32[40,512]{1,0:T(8,128)S(1)} %collective-permute-done.refs_1_.refs_3_, f32[40,512]{1,0:T(8,128)S(1)} %collective-permute-done.1.refs_2_.refs_4_), custom_call_target="tpu_custom_call" | custom-call | flops 3000000000 | bytes 1048576 | tf_op jit(solution)/shard_map/pallas_call | solution.py:82
  33.9 2.7 %collective-permute-start.6 = (f32[24,128]{1,0:T(8,128)S(1)}, f32[24,128]{1,0:T(8,128)S(1)}, u32[]{:S(2)}, u32[]{:S(2)}) collective-permute-start(f32[24,128]{1,0:T(8,128)S(1)} %get-tuple-element.147.refs_1_), channel_id=1, source_target_pairs={{0,16},{1,17},{2,18},{3,19},{4,20},{5,21},{6,22},{7,23},{8,24},{9,... | collective-permute-start | bytes 36872 | tf_op jit(solution)/shard_map/ppermute | solution.py:409
  43.6 2.9 %shard_map.85 = (f32[32,384]{1,0:T(8,128)S(1)}, f32[80,128]{1,0:T(8,128)S(1)}, f32[80,128]{1,0:T(8,128)S(1)}, f32[8,128]{1,0:T(8,128)}) custom-call(s32[1]{0:T(128)S(6)} %select_n.7.core_ref.refs_0_.refs_1_, f32[32,2048]{1,0:T(8,128)S(1)} %get-tuple-element.156.field_ref.refs_10_.refs_12_.refs_8_, bf16[896,2048]{1,0:T(8,128)(2,1)S(1)} %get-tuple-element.113.high_ref.refs_1_, ...), custom_call_target="tpu_custom_call" | custom-call | flops 3000000000 | bytes 1048576 | tf_op jit(solution)/shard_map/pallas_call | solution.py:82
  49.6 2.7 %collective-permute-start.10 = (f32[80,128]{1,0:T(8,128)S(1)}, f32[80,128]{1,0:T(8,128)S(1)}, u32[]{:S(2)}, u32[]{:S(2)}) collective-permute-start(f32[80,128]{1,0:T(8,128)S(1)} %get-tuple-element.160), channel_id=1, source_target_pairs={{0,1},{1,0},{2,3},{3,2},{4,5},{5,4},{6,7},{7,6},{8,9},{9,8},{10,11... | collective-permute-start | bytes 122888 | tf_op jit(solution)/shard_map/ppermute | solution.py:409
  55.6 2.8 %collective-permute-done.11.refs_2_ = f32[80,128]{1,0:T(8,128)S(1)} collective-permute-done((f32[80,128]{1,0:T(8,128)S(1)}, f32[80,128]{1,0:T(8,128)S(1)}, u32[]{:S(2)}, u32[]{:S(2)}) %collective-permute-start.11) | collective-permute-done | bytes 40992 | tf_op jit(solution)/shard_map/ppermute | solution.py:409
  58.6 2.3 %collective-permute-start.12 = (f32[64,128]{1,0:T(8,128)S(1)}, f32[64,128]{1,0:T(8,128)S(1)}, u32[]{:S(2)}, u32[]{:S(2)}) collective-permute-start(f32[64,128]{1,0:T(8,128)S(1)} %get-tuple-element.163.refs_1_), channel_id=1, source_target_pairs={{0,4},{1,5},{2,6},{3,7},{4,0},{5,1},{6,2},{7,3},{8,12},{9,13},{10,... | collective-permute-start | bytes 98312 | tf_op jit(solution)/shard_map/ppermute | solution.py:409
  67.1 4.1 %collective-permute-start.14 = (f32[32,128]{1,0:T(8,128)S(1)}, f32[32,128]{1,0:T(8,128)S(1)}, u32[]{:S(2)}, u32[]{:S(2)}) collective-permute-start(f32[32,128]{1,0:T(8,128)S(1)} %get-tuple-element.165.refs_1_), channel_id=1, source_target_pairs={{0,16},{1,17},{2,18},{3,19},{4,20},{5,21},{6,22},{7,23},{8,24},{9,... | collective-permute-start | bytes 49160 | tf_op jit(solution)/shard_map/ppermute | solution.py:409
  76.4 2.3 %shard_map.93 = (f32[32,384]{1,0:T(8,128)S(1)}, f32[80,128]{1,0:T(8,128)S(1)}, f32[80,128]{1,0:T(8,128)S(1)}, f32[8,128]{1,0:T(8,128)S(1)}) custom-call(s32[1]{0:T(128)S(6)} %select_n.7.core_ref.refs_0_.refs_1_, f32[32,2048]{1,0:T(8,128)S(1)} %get-tuple-element.180.field_ref.refs_7_.refs_9_, bf16[896,2048]{1,0:T(8,128)(2,1)S(1)} %get-tuple-element.113.high_ref.refs_1_, ...), custom_call_target="tpu_custom_call" | custom-call | flops 3000000000 | bytes 1048576 | tf_op jit(solution)/shard_map/pallas_call | solution.py:82
  80.0 3.1 %collective-permute-start.17 = (f32[72,128]{1,0:T(8,128)S(1)}, f32[72,128]{1,0:T(8,128)S(1)}, u32[]{:S(2)}, u32[]{:S(2)}) collective-permute-start(f32[72,128]{1,0:T(8,128)S(1)} %get-tuple-element.176.refs_1_), channel_id=1, source_target_pairs={{0,2},{1,3},{2,0},{3,1},{4,6},{5,7},{6,4},{7,5},{8,10},{9,11},{10,... | collective-permute-start | bytes 110600 | tf_op jit(solution)/shard_map/ppermute | solution.py:409
  92.1 2.2 %collective-permute-done.19.refs_2_ = f32[40,128]{1,0:T(8,128)S(1)} collective-permute-done((f32[40,128]{1,0:T(8,128)S(1)}, f32[40,128]{1,0:T(8,128)S(1)}, u32[]{:S(2)}, u32[]{:S(2)}) %collective-permute-start.19) | collective-permute-done | bytes 20512 | tf_op jit(solution)/shard_map/ppermute | solution.py:409
  94.3 2.4 %collective-permute-start.22 = (f32[24,128]{1,0:T(8,128)S(1)}, f32[24,128]{1,0:T(8,128)S(1)}, u32[]{:S(2)}, u32[]{:S(2)}) collective-permute-start(f32[24,128]{1,0:T(8,128)S(1)} %get-tuple-element.189.refs_1_), channel_id=1, source_target_pairs={{0,16},{1,17},{2,18},{3,19},{4,20},{5,21},{6,22},{7,23},{8,24},{9,... | collective-permute-start | bytes 36872 | tf_op jit(solution)/shard_map/ppermute | solution.py:409
  96.7 2.2 %collective-permute-done.22.refs_2_ = f32[24,128]{1,0:T(8,128)S(1)} collective-permute-done((f32[24,128]{1,0:T(8,128)S(1)}, f32[24,128]{1,0:T(8,128)S(1)}, u32[]{:S(2)}, u32[]{:S(2)}) %collective-permute-start.22) | collective-permute-done | bytes 12320 | tf_op jit(solution)/shard_map/ppermute | solution.py:409
  103.9 2.9 %shard_map.105 = (f32[32,384]{1,0:T(8,128)S(1)}, f32[80,128]{1,0:T(8,128)S(1)}, f32[80,128]{1,0:T(8,128)S(1)}, f32[8,128]{1,0:T(8,128)}) custom-call(s32[1]{0:T(128)S(6)} %select_n.7.core_ref.refs_0_.refs_1_, f32[32,2048]{1,0:T(8,128)S(1)} %get-tuple-element.203.field_ref.refs_10_, bf16[896,2048]{1,0:T(8,128)(2,1)S(1)} %get-tuple-element.113.high_ref.refs_1_, ...), custom_call_target="tpu_custom_call" | custom-call | flops 3000000000 | bytes 1048576 | tf_op jit(solution)/shard_map/pallas_call | solution.py:82
  114.9 2.5 %collective-permute-done.27.refs_2_ = f32[80,128]{1,0:T(8,128)S(1)} collective-permute-done((f32[80,128]{1,0:T(8,128)S(1)}, f32[80,128]{1,0:T(8,128)S(1)}, u32[]{:S(2)}, u32[]{:S(2)}) %collective-permute-start.27) | collective-permute-done | bytes 40992 | tf_op jit(solution)/shard_map/ppermute | solution.py:409
  117.7 2.3 %collective-permute-start.28 = (f32[64,128]{1,0:T(8,128)S(1)}, f32[64,128]{1,0:T(8,128)S(1)}, u32[]{:S(2)}, u32[]{:S(2)}) collective-permute-start(f32[64,128]{1,0:T(8,128)S(1)} %get-tuple-element.214.refs_1_), channel_id=1, source_target_pairs={{0,4},{1,5},{2,6},{3,7},{4,0},{5,1},{6,2},{7,3},{8,12},{9,13},{10,... | collective-permute-start | bytes 98312 | tf_op jit(solution)/shard_map/ppermute | solution.py:409
  122.1 2.7 %collective-permute-start.29 = (f32[48,128]{1,0:T(8,128)S(1)}, f32[48,128]{1,0:T(8,128)S(1)}, u32[]{:S(2)}, u32[]{:S(2)}) collective-permute-start(f32[48,128]{1,0:T(8,128)S(1)} %get-tuple-element.215.refs_1_), channel_id=1, source_target_pairs={{0,8},{1,9},{2,10},{3,11},{4,12},{5,13},{6,14},{7,15},{8,0},{9,1},... | collective-permute-start | bytes 73736 | tf_op jit(solution)/shard_map/ppermute | solution.py:409
  126.9 4.1 %collective-permute-start.30 = (f32[32,128]{1,0:T(8,128)S(1)}, f32[32,128]{1,0:T(8,128)S(1)}, u32[]{:S(2)}, u32[]{:S(2)}) collective-permute-start(f32[32,128]{1,0:T(8,128)S(1)} %get-tuple-element.216.refs_1_), channel_id=1, source_target_pairs={{0,16},{1,17},{2,18},{3,19},{4,20},{5,21},{6,22},{7,23},{8,24},{9,... | collective-permute-start | bytes 49160 | tf_op jit(solution)/shard_map/ppermute | solution.py:409
  134.5 2.2 %shard_map.112 = (f32[32,2048]{1,0:T(8,128)}, f32[32,2048]{1,0:T(8,128)}) custom-call(s32[1]{0:T(128)S(6)} %select_n.7.core_ref.refs_0_.refs_1_, bf16[896,2048]{1,0:T(8,128)(2,1)S(1)} %get-tuple-element.113.high_ref.refs_1_, bf16[896,2048]{1,0:T(8,128)(2,1)S(1)} %copy-done.1, f32[32,2048]{1,0:T(8,128)S(1)} %get-tuple-element.208.refs_3_, ...), custom_call_target="tpu_custom_call" | custom-call | flops 1500000000 | bytes 1048576 | tf_op jit(solution)/shard_map/pallas_call | solution.py:82
  (98 shorter events, 65.8 us)
Async XLA Ops:
  13.0 16.4 %collective-permute-start = (f32[40,512]{1,0:T(8,128)S(1)}, f32[40,512]{1,0:T(8,128)S(1)}, u32[]{:S(2)}, u32[]{:S(2)}) collective-permute-start(f32[40,512]{1,0:T(8,128)S(1)} %get-tuple-element.115), channel_id=1, source_target_pairs={{0,1},{1,0},{2,3},{3,2},{4,5},{5,4},{6,7},{7,6},{8,9},{9,8},{10,11... | collective-permute-start | bytes 245768 | tf_op jit(solution)/shard_map/ppermute | solution.py:409
  13.1 16.3 %collective-permute-start.1 = (f32[40,512]{1,0:T(8,128)S(1)}, f32[40,512]{1,0:T(8,128)S(1)}, u32[]{:S(2)}, u32[]{:S(2)}) collective-permute-start(f32[40,512]{1,0:T(8,128)S(1)} %get-tuple-element.116), channel_id=1, source_target_pairs={{1,2},{3,4},{5,6},{7,8},{9,10},{11,12},{13,14},{15,16},{17,18},{19... | collective-permute-start | bytes 245768 | tf_op jit(solution)/shard_map/ppermute | solution.py:414
  13.8 7.3 %collective-permute-start.3 = (f32[72,128]{1,0:T(8,128)S(1)}, f32[72,128]{1,0:T(8,128)S(1)}, u32[]{:S(2)}, u32[]{:S(2)}) collective-permute-start(f32[72,128]{1,0:T(8,128)S(1)} %get-tuple-element.120.refs_1_), channel_id=1, source_target_pairs={{0,2},{1,3},{2,0},{3,1},{4,6},{5,7},{6,4},{7,5},{8,10},{9,11},{10,... | collective-permute-start | bytes 110600 | tf_op jit(solution)/shard_map/ppermute | solution.py:409
  21.1 6.0 %collective-permute-start.4 = (f32[56,128]{1,0:T(8,128)S(1)}, f32[56,128]{1,0:T(8,128)S(1)}, u32[]{:S(2)}, u32[]{:S(2)}) collective-permute-start(f32[56,128]{1,0:T(8,128)S(1)} %get-tuple-element.126.refs_1_), channel_id=1, source_target_pairs={{0,4},{1,5},{2,6},{3,7},{4,0},{5,1},{6,2},{7,3},{8,12},{9,13},{10,... | collective-permute-start | bytes 86024 | tf_op jit(solution)/shard_map/ppermute | solution.py:409
  27.2 6.7 %collective-permute-start.5 = (f32[40,128]{1,0:T(8,128)S(1)}, f32[40,128]{1,0:T(8,128)S(1)}, u32[]{:S(2)}, u32[]{:S(2)}) collective-permute-start(f32[40,128]{1,0:T(8,128)S(1)} %get-tuple-element.132.refs_1_), channel_id=1, source_target_pairs={{0,8},{1,9},{2,10},{3,11},{4,12},{5,13},{6,14},{7,15},{8,0},{9,1},... | collective-permute-start | bytes 61448 | tf_op jit(solution)/shard_map/ppermute | solution.py:409
  33.9 4.7 %collective-permute-start.6 = (f32[24,128]{1,0:T(8,128)S(1)}, f32[24,128]{1,0:T(8,128)S(1)}, u32[]{:S(2)}, u32[]{:S(2)}) collective-permute-start(f32[24,128]{1,0:T(8,128)S(1)} %get-tuple-element.147.refs_1_), channel_id=1, source_target_pairs={{0,16},{1,17},{2,18},{3,19},{4,20},{5,21},{6,22},{7,23},{8,24},{9,... | collective-permute-start | bytes 36872 | tf_op jit(solution)/shard_map/ppermute | solution.py:409
  46.4 5.9 %collective-permute-start.8 = (f32[32,512]{1,0:T(8,128)S(1)}, f32[32,512]{1,0:T(8,128)S(1)}, u32[]{:S(2)}, u32[]{:S(2)}) collective-permute-start(f32[32,512]{1,0:T(8,128)S(1)} %get-tuple-element.154), channel_id=1, source_target_pairs={{0,1},{1,0},{2,3},{3,2},{4,5},{5,4},{6,7},{7,6},{8,9},{9,8},{10,11... | collective-permute-start | bytes 196616 | tf_op jit(solution)/shard_map/ppermute | solution.py:409
  47.0 5.4 %collective-permute-start.9 = (f32[32,512]{1,0:T(8,128)S(1)}, f32[32,512]{1,0:T(8,128)S(1)}, u32[]{:S(2)}, u32[]{:S(2)}) collective-permute-start(f32[32,512]{1,0:T(8,128)S(1)} %get-tuple-element.155), channel_id=1, source_target_pairs={{1,2},{3,4},{5,6},{7,8},{9,10},{11,12},{13,14},{15,16},{17,18},{19... | collective-permute-start | bytes 196616 | tf_op jit(solution)/shard_map/ppermute | solution.py:414
  49.6 4.2 %collective-permute-start.10 = (f32[80,128]{1,0:T(8,128)S(1)}, f32[80,128]{1,0:T(8,128)S(1)}, u32[]{:S(2)}, u32[]{:S(2)}) collective-permute-start(f32[80,128]{1,0:T(8,128)S(1)} %get-tuple-element.160), channel_id=1, source_target_pairs={{0,1},{1,0},{2,3},{3,2},{4,5},{5,4},{6,7},{7,6},{8,9},{9,8},{10,11... | collective-permute-start | bytes 122888 | tf_op jit(solution)/shard_map/ppermute | solution.py:409
  54.1 4.3 %collective-permute-start.11 = (f32[80,128]{1,0:T(8,128)S(1)}, f32[80,128]{1,0:T(8,128)S(1)}, u32[]{:S(2)}, u32[]{:S(2)}) collective-permute-start(f32[80,128]{1,0:T(8,128)S(1)} %get-tuple-element.162.refs_1_), channel_id=1, source_target_pairs={{0,2},{1,3},{2,0},{3,1},{4,6},{5,7},{6,4},{7,5},{8,10},{9,11},{10,... | collective-permute-start | bytes 122888 | tf_op jit(solution)/shard_map/ppermute | solution.py:409
  58.6 4.2 %collective-permute-start.12 = (f32[64,128]{1,0:T(8,128)S(1)}, f32[64,128]{1,0:T(8,128)S(1)}, u32[]{:S(2)}, u32[]{:S(2)}) collective-permute-start(f32[64,128]{1,0:T(8,128)S(1)} %get-tuple-element.163.refs_1_), channel_id=1, source_target_pairs={{0,4},{1,5},{2,6},{3,7},{4,0},{5,1},{6,2},{7,3},{8,12},{9,13},{10,... | collective-permute-start | bytes 98312 | tf_op jit(solution)/shard_map/ppermute | solution.py:409
  63.0 3.9 %collective-permute-start.13 = (f32[48,128]{1,0:T(8,128)S(1)}, f32[48,128]{1,0:T(8,128)S(1)}, u32[]{:S(2)}, u32[]{:S(2)}) collective-permute-start(f32[48,128]{1,0:T(8,128)S(1)} %get-tuple-element.164.refs_1_), channel_id=1, source_target_pairs={{0,8},{1,9},{2,10},{3,11},{4,12},{5,13},{6,14},{7,15},{8,0},{9,1},... | collective-permute-start | bytes 73736 | tf_op jit(solution)/shard_map/ppermute | solution.py:409
  67.1 6.0 %collective-permute-start.14 = (f32[32,128]{1,0:T(8,128)S(1)}, f32[32,128]{1,0:T(8,128)S(1)}, u32[]{:S(2)}, u32[]{:S(2)}) collective-permute-start(f32[32,128]{1,0:T(8,128)S(1)} %get-tuple-element.165.refs_1_), channel_id=1, source_target_pairs={{0,16},{1,17},{2,18},{3,19},{4,20},{5,21},{6,22},{7,23},{8,24},{9,... | collective-permute-start | bytes 49160 | tf_op jit(solution)/shard_map/ppermute | solution.py:409
  78.9 11.9 %collective-permute-start.20 = (f32[32,512]{1,0:T(8,128)S(1)}, f32[32,512]{1,0:T(8,128)S(1)}, u32[]{:S(2)}, u32[]{:S(2)}) collective-permute-start(f32[32,512]{1,0:T(8,128)S(1)} %get-tuple-element.183), channel_id=1, source_target_pairs={{0,1},{1,0},{2,3},{3,2},{4,5},{5,4},{6,7},{7,6},{8,9},{9,8},{10,11... | collective-permute-start | bytes 196616 | tf_op jit(solution)/shard_map/ppermute | solution.py:409
  79.3 11.5 %collective-permute-start.21 = (f32[32,512]{1,0:T(8,128)S(1)}, f32[32,512]{1,0:T(8,128)S(1)}, u32[]{:S(2)}, u32[]{:S(2)}) collective-permute-start(f32[32,512]{1,0:T(8,128)S(1)} %get-tuple-element.184), channel_id=1, source_target_pairs={{1,2},{3,4},{5,6},{7,8},{9,10},{11,12},{13,14},{15,16},{17,18},{19... | collective-permute-start | bytes 196616 | tf_op jit(solution)/shard_map/ppermute | solution.py:414
  80.0 6.7 %collective-permute-start.17 = (f32[72,128]{1,0:T(8,128)S(1)}, f32[72,128]{1,0:T(8,128)S(1)}, u32[]{:S(2)}, u32[]{:S(2)}) collective-permute-start(f32[72,128]{1,0:T(8,128)S(1)} %get-tuple-element.176.refs_1_), channel_id=1, source_target_pairs={{0,2},{1,3},{2,0},{3,1},{4,6},{5,7},{6,4},{7,5},{8,10},{9,11},{10,... | collective-permute-start | bytes 110600 | tf_op jit(solution)/shard_map/ppermute | solution.py:409
  86.7 3.9 %collective-permute-start.18 = (f32[56,128]{1,0:T(8,128)S(1)}, f32[56,128]{1,0:T(8,128)S(1)}, u32[]{:S(2)}, u32[]{:S(2)}) collective-permute-start(f32[56,128]{1,0:T(8,128)S(1)} %get-tuple-element.179.refs_1_), channel_id=1, source_target_pairs={{0,4},{1,5},{2,6},{3,7},{4,0},{5,1},{6,2},{7,3},{8,12},{9,13},{10,... | collective-permute-start | bytes 86024 | tf_op jit(solution)/shard_map/ppermute | solution.py:409
  94.3 4.6 %collective-permute-start.22 = (f32[24,128]{1,0:T(8,128)S(1)}, f32[24,128]{1,0:T(8,128)S(1)}, u32[]{:S(2)}, u32[]{:S(2)}) collective-permute-start(f32[24,128]{1,0:T(8,128)S(1)} %get-tuple-element.189.refs_1_), channel_id=1, source_target_pairs={{0,16},{1,17},{2,18},{3,19},{4,20},{5,21},{6,22},{7,23},{8,24},{9,... | collective-permute-start | bytes 36872 | tf_op jit(solution)/shard_map/ppermute | solution.py:409
  106.8 4.8 %collective-permute-start.24 = (f32[32,512]{1,0:T(8,128)S(1)}, f32[32,512]{1,0:T(8,128)S(1)}, u32[]{:S(2)}, u32[]{:S(2)}) collective-permute-start(f32[32,512]{1,0:T(8,128)S(1)} %get-tuple-element.201), channel_id=1, source_target_pairs={{0,1},{1,0},{2,3},{3,2},{4,5},{5,4},{6,7},{7,6},{8,9},{9,8},{10,11... | collective-permute-start | bytes 196616 | tf_op jit(solution)/shard_map/ppermute | solution.py:409
  106.9 4.6 %collective-permute-start.25 = (f32[32,512]{1,0:T(8,128)S(1)}, f32[32,512]{1,0:T(8,128)S(1)}, u32[]{:S(2)}, u32[]{:S(2)}) collective-permute-start(f32[32,512]{1,0:T(8,128)S(1)} %get-tuple-element.202), channel_id=1, source_target_pairs={{1,2},{3,4},{5,6},{7,8},{9,10},{11,12},{13,14},{15,16},{17,18},{19... | collective-permute-start | bytes 196616 | tf_op jit(solution)/shard_map/ppermute | solution.py:414
  113.3 4.1 %collective-permute-start.27 = (f32[80,128]{1,0:T(8,128)S(1)}, f32[80,128]{1,0:T(8,128)S(1)}, u32[]{:S(2)}, u32[]{:S(2)}) collective-permute-start(f32[80,128]{1,0:T(8,128)S(1)} %get-tuple-element.213.refs_1_), channel_id=1, source_target_pairs={{0,2},{1,3},{2,0},{3,1},{4,6},{5,7},{6,4},{7,5},{8,10},{9,11},{10,... | collective-permute-start | bytes 122888 | tf_op jit(solution)/shard_map/ppermute | solution.py:409
  117.7 4.2 %collective-permute-start.28 = (f32[64,128]{1,0:T(8,128)S(1)}, f32[64,128]{1,0:T(8,128)S(1)}, u32[]{:S(2)}, u32[]{:S(2)}) collective-permute-start(f32[64,128]{1,0:T(8,128)S(1)} %get-tuple-element.214.refs_1_), channel_id=1, source_target_pairs={{0,4},{1,5},{2,6},{3,7},{4,0},{5,1},{6,2},{7,3},{8,12},{9,13},{10,... | collective-permute-start | bytes 98312 | tf_op jit(solution)/shard_map/ppermute | solution.py:409
  122.1 4.6 %collective-permute-start.29 = (f32[48,128]{1,0:T(8,128)S(1)}, f32[48,128]{1,0:T(8,128)S(1)}, u32[]{:S(2)}, u32[]{:S(2)}) collective-permute-start(f32[48,128]{1,0:T(8,128)S(1)} %get-tuple-element.215.refs_1_), channel_id=1, source_target_pairs={{0,8},{1,9},{2,10},{3,11},{4,12},{5,13},{6,14},{7,15},{8,0},{9,1},... | collective-permute-start | bytes 73736 | tf_op jit(solution)/shard_map/ppermute | solution.py:409
  126.9 5.8 %collective-permute-start.30 = (f32[32,128]{1,0:T(8,128)S(1)}, f32[32,128]{1,0:T(8,128)S(1)}, u32[]{:S(2)}, u32[]{:S(2)}) collective-permute-start(f32[32,128]{1,0:T(8,128)S(1)} %get-tuple-element.216.refs_1_), channel_id=1, source_target_pairs={{0,16},{1,17},{2,18},{3,19},{4,20},{5,21},{6,22},{7,23},{8,24},{9,... | collective-permute-start | bytes 49160 | tf_op jit(solution)/shard_map/ppermute | solution.py:409
  (14 other events, 37.3 us)
where the time goes:
time: 137 us
  Pallas kernels  55.8 us (41%)
  starting transfers between devices  47 us (34%)
  waiting for transfers between devices  29.1 us (21%)
  local copies, waits for them, and re-layouts  3.92 us (3%)
    pallas_call x44, Pallas kernels, call(): pl.pallas_call(body, out_shape=outs, in_specs=[whole(pltpu.SMEM)] * scala...  50.2 us
    ppermute x28, starting transfers between devices, swap(): lax.ppermute(value, BOTH, [(source, source ^ 1 << bit) for source in rang...  44.2 us
    ppermute x28, waiting for transfers between devices, swap(): lax.ppermute(value, BOTH, [(source, source ^ 1 << bit) for source in rang...  29 us
    pallas_call x1, Pallas kernels, per_device(): pl.pallas_call(functools.partial(setup_kernel, pairs), out_shape=[bf16(ha...  5.53 us
    unnamed x13, local copies, waits for them, and re-layouts  3.92 us
    ppermute x4, starting transfers between devices, halo(): lax.ppermute(other, BOTH, outward + [(target, source) for source, target...  2.79 us
  transfers between devices with their start and end apart: 32, of which 18 were waited for; matrix products, arithmetic and copies ran while one was open for 0% of the time, Pallas kernels for 19%

commit v1 on v0

--- a/solution.py
+++ b/solution.py
@@ -251,39 +251,71 @@
     tile_ref[...] = sums_tile([totals[pair] for pair in PAIRS], rows, PRODUCTS_TILE)
 
 
-def combine_kernel(products, bit, cluster, *refs):
-    refs = list(refs)
-    core_ref, mine_ref, other_ref = refs[:3]
-    refs = refs[3:]
-    tile_ref = refs.pop(0) if bit == 0 else None
-    if products:
-        field_ref, direction_ref = refs[:2]
-        refs = refs[2:]
-    *level_refs, next_ref, level_ref = refs
+def first_combine_kernel(products, cluster, *refs):
+    core_ref, mine_ref, other_ref, tile_ref = refs[:4]
+    message_ref, level_ref = refs[-2:]
     own = level_ref.shape[0]
-    depth = PRODUCTS_TILE if products else NORM_TILE
+    depth = tile_ref.shape[0]
     total = mine_ref[...] + other_ref[...]
-    if bit == 0:
-        tile = tile_ref[...]
-    else:
-        tile = total[total.shape[0] - depth :]
-        total = total[: total.shape[0] - depth]
     level = total[:own]
     level_ref[...] = level
+    tile = tile_ref[...]
     if products:
-        here = slice(bit * own, (bit + 1) * own)
-        partners = [field_ref[here], level, direction_ref[here]]
+        partners = [refs[4][:own], level, refs[5][:own]]
         columns = [row_sum(level * partner) * (1.0 / cluster) for partner in partners]
         tile = tile + level_terms(core_ref[0], columns, 2 * own, depth)
     left = total.shape[0] - own
+    message_ref[:left] = total[own:]
+    message_ref[left:] = tile
+
+
+def combine_kernel(products, bits, clusters, *refs):
+    refs = list(refs)
+    core_ref, mine_ref = refs[:2]
+    got = [ref[...] for ref in refs[2 : 2 + 2 ** len(bits) - 1]]
+    refs = refs[1 + 2 ** len(bits) :]
+    sibling_ref = refs.pop() if len(bits) == 2 else None
+    level_out = [refs.pop() for _ in bits][::-1]
+    next_ref = refs.pop()
+    own = level_out[0].shape[0]
+    depth = PRODUCTS_TILE if products else NORM_TILE
+    near = mine_ref[...] + got[0]
+    total = near
+    pairs = [(near[:own], bits[0], 0, clusters[0])]
+    if len(bits) == 2:
+        far = got[1] + got[2]
+        total = near + far
+        sibling = far[:own]
+        sibling_ref[...] = sibling
+        pairs.append((sibling, None, 1, clusters[0]))
+        pairs.append((total[own : 2 * own], bits[1], 0, clusters[1]))
+    for ref, pair in zip(level_out, pairs[:: 2 if len(bits) == 2 else 1]):
+        ref[...] = pair[0]
+    tile = total[total.shape[0] - depth :]
+    if products:
+        r_ref, d_ref = refs[:2]
+        refs = refs[2:]
+        siblings = [refs.pop(0), refs.pop(0)] if len(bits) == 2 else []
+        columns = [jnp.zeros((own, 1), jnp.float32)] * 3
+        for level, bit, kind, cluster in pairs:
+            if kind:
+                partners = [siblings[0][...], level, siblings[1][...]]
+            else:
+                here = slice(bit * own, (bit + 1) * own)
+                partners = [r_ref[here], level, d_ref[here]]
+            terms = [row_sum(level * partner) * (1.0 / cluster) for partner in partners]
+            columns = [column + term for column, term in zip(columns, terms)]
+        tile = tile + level_terms(core_ref[0], columns, 2 * own, depth)
+    left = total.shape[0] - depth - len(bits) * own
     if left:
-        next_ref[:left] = total[own:]
+        next_ref[:left] = total[len(bits) * own : len(bits) * own + left]
         next_ref[left:] = tile
     else:
-        for index, ref in enumerate(level_refs):
+        for index, ref in enumerate(refs):
             next_ref[index * own : (index + 1) * own] = ref[...]
-        next_ref[bit * own : (bit + 1) * own] = level
-        next_ref[(bit + 1) * own :] = tile
+        for bit, pair in zip(bits, pairs[:: 2 if len(bits) == 2 else 1]):
+            next_ref[bit * own : (bit + 1) * own] = pair[0]
+        next_ref[next_ref.shape[0] - depth :] = tile
 
 
 def up_parts(core, mine_ref, other_ref, local_ref, rows, width, depth):
@@ -314,7 +346,7 @@
     send_ref[...] = chosen(core, tail, head)
 
 
-def residual_up_kernel(first, *refs):
+def residual_up_kernel(first, siblings, *refs):
     core_ref, high_ref, low_ref, near_ref, mine_ref, other_ref, local_ref = refs[:7]
     refs = refs[7:]
     if first:
@@ -322,7 +354,11 @@
         q_ref = image_ref
     else:
         field_ref, old_d_ref, old_q_ref, old_skel_ref, old_local_ref, old_state_ref = refs[:6]
-        image_ref, state_ref, paired_ref, send_ref, d_ref, q_ref, skel_ref, new_local_ref = refs[6:]
+        r_siblings = refs[6 : 6 + siblings]
+        d_siblings = refs[6 + siblings : 6 + 2 * siblings]
+        refs = refs[6 + 2 * siblings :]
+        image_ref, state_ref, paired_ref, send_ref, d_ref, q_ref, skel_ref, new_local_ref = refs[:8]
+        new_siblings = refs[8:]
     core = core_ref[0]
     rows, width = near_ref.shape
     half = width // 2
@@ -343,9 +379,12 @@
         crossing = rows_in // (rows // 2)
         skel_ref[...] = mine_ref[:rows_in] + own_rows(core, ratio, crossing) * old_skel_ref[...]
         new_local_ref[...] = local_ref[...] + ratio * old_local_ref[...]
-
-
-def image_up_kernel(first, last, *refs):
+        own_ratio = own_rows(core, ratio, 1)
+        for new_ref, r_ref, d_ref in zip(new_siblings, r_siblings, d_siblings):
+            new_ref[...] = r_ref[...] + own_ratio * d_ref[...]
+
+
+def image_up_kernel(first, last, siblings, *refs):
     core_ref, high_ref, low_ref, near_ref, mine_ref, other_ref, local_ref = refs[:7]
     r_ref, w_ref, d_ref, q_ref, state_ref = refs[7:12]
     refs = refs[12:]
@@ -354,10 +393,14 @@
         refs = refs[1:]
     if not last:
         r_skel_ref, d_skel_ref, r_local_ref, d_local_ref = refs[:4]
-        refs = refs[4:]
+        r_siblings, q_siblings, d_siblings = [
+            refs[4 + index * siblings : 4 + (index + 1) * siblings] for index in range(3)
+        ]
+        refs = refs[4 + 3 * siblings :]
     new_solution_ref, new_r_ref = refs[:2]
     if not last:
-        new_d_ref, new_q_ref, new_skel_ref, new_local_ref, new_state_ref, paired_ref, send_ref = refs[2:]
+        new_d_ref, new_q_ref, new_skel_ref, new_local_ref, new_state_ref, paired_ref, send_ref = refs[2:9]
+        new_siblings = refs[9:]
     core = core_ref[0]
     rows, width = near_ref.shape
     half = width // 2
@@ -390,6 +433,9 @@
         r_skel = r_skel_ref[:rows_in] - own_rows(core, step, crossing) * mine_ref[:rows_in]
         new_skel_ref[...] = r_skel + own_rows(core, ratio, crossing) * d_skel_ref[:rows_in]
         new_local_ref[...] = r_local_ref[...] - step * local_ref[...] + ratio * d_local_ref[...]
+        own_step, own_ratio = own_rows(core, step, 1), own_rows(core, ratio, 1)
+        for new_ref, r_ref, q_ref, d_ref in zip(new_siblings, r_siblings, q_siblings, d_siblings):
+            new_ref[...] = r_ref[...] - own_step * q_ref[...] + own_ratio * d_ref[...]
         new_state_ref[...] = in_lanes([new_norm], (rows, LANES))
         put_edges(core, new_r_ref, paired_ref, send_ref)
 
@@ -405,13 +451,16 @@
     core = place % 2
     nugget = nugget[None, :]
 
-    def swap(value, bit):
-        return lax.ppermute(value, BOTH, [(source, source ^ (1 << bit)) for source in range(devices)])
+    stages = [list(range(bit, min(bit + 2, crossing))) for bit in range(1, crossing, 2)]
+    siblings = sum(len(bits) == 2 for bits in stages)
+
+    def swap(value, mask):
+        return lax.ppermute(value, BOTH, [(source, source ^ mask) for source in range(devices)])
 
     def halo(paired, other):
         outward = [(index, index + 1) for index in range(1, devices - 1, 2)]
         ends = [(0, 0), (devices - 1, devices - 1)]
-        return swap(paired, 0), lax.ppermute(other, BOTH, outward + [(target, source) for source, target in outward] + ends)
+        return swap(paired, 1), lax.ppermute(other, BOTH, outward + [(target, source) for source, target in outward] + ends)
 
     def down(field):
         shapes = [f32(rows, LOCAL * LANES)] + [f32(crossing * own, LANES)] * 2 + [f32(NORM_TILE, LANES)]
@@ -427,26 +476,45 @@
         args = [place, core, near_ids, *edges, *outside, front, back, *more]
         return call(functools.partial(edge_kernel, bool(more)), shapes, *args, scalars=3, flops=FLOPS // 3)
 
-    def chain(products, keep, got, tile, beside_steps, *skeletons):
+    def chain(products, keep, got, tile, beside_steps, r_skel=None, d_skel=None, r_sib=(), d_sib=()):
         depth = PRODUCTS_TILE if products else NORM_TILE
-        done = []
         results = []
-        message = keep
-        for bit in range(crossing):
-            left = crossing - bit - 1
-            args = [core, message, got] + ([tile] if bit == 0 else []) + list(skeletons) + (done if left == 0 else [])
-            message, level = call(
-                functools.partial(combine_kernel, products, bit, width * (2 << bit)),
-                [f32((left or crossing) * own + depth, LANES), f32(own, LANES)],
+        both = [r_skel, d_skel] if products else []
+        message, level = call(
+            functools.partial(first_combine_kernel, products, 2 * width),
+            [f32((crossing - 1) * own + depth, LANES), f32(own, LANES)],
+            core,
+            keep,
+            got,
+            tile,
+            *both,
+            scalars=1,
+        )
+        done, kept = [level], []
+        for index in range(len(stages) + 1):
+            bits = stages[index] if index < len(stages) else []
+            masks = [sum(1 << bit for at, bit in enumerate(bits) if pick >> at & 1) for pick in range(1, 2 ** len(bits))]
+            got = [swap(message, mask) for mask in masks or [1]]
+            if index < len(beside_steps):
+                *got, result = lax.optimization_barrier((*got, beside_steps[index](message)))
+                results.append(result)
+            if not bits:
+                break
+            left = crossing - bits[-1] - 1
+            paired = len(bits) == 2
+            args = [core, message, *got, *both]
+            if products and paired:
+                args = args + [r_sib[len(kept)], d_sib[len(kept)]]
+            message, *levels_out = call(
+                functools.partial(combine_kernel, products, bits, [width * (2 << bit) for bit in bits]),
+                [f32((left or crossing) * own + depth, LANES)] + [f32(own, LANES)] * (3 if paired else 1),
                 *args,
+                *([] if left else done),
                 scalars=1,
             )
-            done.append(level)
-            got = swap(message, bit + 1 if left else 0)
-            if bit < len(beside_steps):
-                got, result = lax.optimization_barrier((got, beside_steps[bit](message)))
-                results.append(result)
-        return message, got, results
+            done = done + levels_out[: len(bits)]
+            kept = kept + levels_out[len(bits) :]
+        return message, got[0], results, kept
 
     edges = halo(*call(edges_kernel, [f32(rows + 8, LEAF)] * 2, core, rhs, coords, scalars=1))
     turned = coords.T
@@ -454,11 +522,11 @@
     pairs = [(leaf, leaf) for leaf in range(half)]
     *front_diagonal, high, low = pl.pallas_call(
         functools.partial(setup_kernel, pairs),
-        out_shape=[bf16(half, LEAF, LEAF)] * 2 + [bf16(levels * LANES, width)] * 2,
+        out_shape=[bf16(half, LEAF, LEAF)] * 2 + [pltpu.VMEM((levels * LANES, width), jnp.bfloat16)] * 2,
         in_specs=[whole(), whole(), whole(pltpu.HBM)],
         out_specs=[whole()] * 4,
         scratch_shapes=[pltpu.VMEM(basis.shape, jnp.float32), pltpu.SemaphoreType.DMA((levels,))],
-        compiler_params=pltpu.CompilerParams(vmem_limit_bytes=46 * 2**20),
+        compiler_params=pltpu.CompilerParams(vmem_limit_bytes=44 * 2**20),
         cost_estimate=pl.CostEstimate(flops=FLOPS, bytes_accessed=2**20, transcendentals=0),
     )(coords, turned, basis)
     diagonal = [front_diagonal, None]
@@ -467,12 +535,15 @@
     def after(message, *values):
         return lax.optimization_barrier((message, *values))[1:]
 
-    def late_matrices(pairs):
-        def run(message):
-            shapes = [bf16(len(pairs), LEAF, LEAF)] * 2
-            return call(functools.partial(fill_matrices, pairs), shapes, *after(message, coords, turned), flops=FLOPS)
-
-        return run
+    def late_matrices(message):
+        groups = [[(leaf, leaf) for leaf in range(half, leaves)], [(leaf, leaf + 1) for leaf in range(leaves - 1)]]
+
+        def body(lane_ref, sub_ref, *refs):
+            for index, group in enumerate(groups):
+                fill_matrices(group, lane_ref, sub_ref, *refs[2 * index : 2 * index + 2])
+
+        shapes = [bf16(len(group), LEAF, LEAF) for group in groups for _ in range(2)]
+        return call(body, shapes, *after(message, coords, turned), flops=2 * FLOPS)
 
     def late_edge_matrices(message):
         def body(core_ref, *refs):
@@ -485,62 +556,59 @@
     for step in range(0, ITERS, 2):
         first, last = step == 0, step + 2 == ITERS
         r_local, keep, part, tile = down(r)
-        got = swap(part, 0)
+        got = swap(part, 1)
         if first:
-            work = [
-                late_matrices([(leaf, leaf) for leaf in range(half, leaves)]),
-                late_matrices([(leaf, leaf + 1) for leaf in range(leaves - 1)]),
-                late_edge_matrices,
-            ]
-            message, got, results = chain(False, keep, got, tile, work)
-            diagonal[1], beside, outside = results
+            message, got, results, r_sib = chain(False, keep, got, tile, [late_matrices, late_edge_matrices])
+            diagonal[1], beside = results[0][:2], results[0][2:]
+            outside = results[1]
             (near,) = edge(edges, inner(0, r), inner(1, r))
         else:
             fronts = []
 
-            def front_work(message):
-                fronts.append(inner(0, *after(message, r)))
-                return fronts[0]
-
-            def back_work(message):
-                fronts.append(inner(1, *after(message, r)))
-                return fronts[1]
+            def inner_work(message):
+                fronts.extend(inner(half, *after(message, r)) for half in range(2))
+                return fronts
 
             def edge_work(message):
                 return edge(edges, *after(message, *fronts))[0]
 
-            message, got, results = chain(False, keep, got, tile, [front_work, back_work, edge_work])
-            near = results[2]
+            message, got, results, r_sib = chain(False, keep, got, tile, [inner_work, edge_work])
+            near = results[1]
         args = [core, high, low, near, message, got, r_local]
         outs = [f32(rows, width), f32(rows, LANES)] + [f32(rows, LEAF)] * 2
         if first:
             w, state, *edges = call(
-                functools.partial(residual_up_kernel, True), outs, *args, scalars=1, flops=FLOPS // 2
+                functools.partial(residual_up_kernel, True, 0), outs, *args, scalars=1, flops=FLOPS // 2
             )
-            d, q, d_skel, d_local = r, w, message, r_local
+            d, q, d_skel, d_local, d_sib = r, w, message, r_local, r_sib
         else:
             outs = outs + [f32(rows, width)] * 2 + [f32(crossing * own, LANES), f32(rows, LOCAL * LANES)]
-            w, state, *edges, d, q, d_skel, d_local = call(
-                functools.partial(residual_up_kernel, False), outs, *args, r, *carried, scalars=1, flops=FLOPS // 2
+            outs = outs + [f32(own, LANES)] * siblings
+            body = functools.partial(residual_up_kernel, False, siblings)
+            args = args + [r, *carried, *r_sib, *d_sib]
+            w, state, edge_paired, edge_other, d, q, d_skel, d_local, *d_sib = call(
+                body, outs, *args, scalars=1, flops=FLOPS // 2
             )
+            edges = (edge_paired, edge_other)
         r_skel = message
         edges = halo(*edges)
         q_local, keep, part, _ = down(q)
-        got = swap(part, 0)
+        got = swap(part, 1)
         near, tile = edge(edges, inner(0, q), inner(1, q), r, q, d, w, r_local, q_local, d_local)
-        message, got, _ = chain(True, keep, got, tile, [], r_skel, d_skel)
+        message, got, _, q_sib = chain(True, keep, got, tile, [], r_skel, d_skel, r_sib, d_sib)
         args = [core, high, low, near, message, got, q_local, r, w, d, q, state]
-        args = args + ([] if first else [solution]) + ([] if last else [r_skel, d_skel, r_local, d_local])
+        args = args + ([] if first else [solution]) + ([] if last else [r_skel, d_skel, r_local, d_local, *r_sib, *q_sib, *d_sib])
         outs = [f32(rows, width)] * 2
         if not last:
             outs = outs + [f32(rows, width)] * 2 + [f32(crossing * own, LANES), f32(rows, LOCAL * LANES)]
-            outs = outs + [f32(rows, LANES)] + [f32(rows, LEAF)] * 2
+            outs = outs + [f32(rows, LANES)] + [f32(rows, LEAF)] * 2 + [f32(own, LANES)] * siblings
         solution, r, *rest = call(
-            functools.partial(image_up_kernel, first, last), outs, *args, scalars=1, flops=FLOPS // 2
+            functools.partial(image_up_kernel, first, last, siblings), outs, *args, scalars=1, flops=FLOPS // 2
         )
         if not last:
             carried = rest[:5]
-            edges = halo(*rest[5:])
+            edges = halo(*rest[5:7])
+            d_sib = rest[7:]
     return (solution, r)
 
 

time: 137 us -> 128 us (0.934)
  waiting for transfers between devices: 29.1 us -> 18.9 us
  starting transfers between devices: 47 us -> 50 us
    ppermute x28 -> x36, waiting for transfers between devices: 29 us -> 18.9 us  [swap(): lax.ppermute(value, BOTH, [(source, source ^ mask) for source in range(de...]
    ppermute x28 -> x36, starting transfers between devices: 44.2 us -> 47 us  [swap(): lax.ppermute(value, BOTH, [(source, source ^ mask) for source in range(de...]
    pallas_call x44 -> x35, Pallas kernels: 50.2 us -> 49.9 us  [call(): pl.pallas_call(body, out_shape=outs, in_specs=[whole(pltpu.SMEM)] * scala...]
  transfers between devices with their start and end apart: 32 -> 40, of which waited for: 18 -> 15; matrix products, arithmetic and copies ran while one was open for 0% -> 0% of each run, Pallas kernels for 19% -> 20%
where the time goes in v1:
time: 128 us
  Pallas kernels  54.9 us (43%)
  starting transfers between devices  50 us (39%)
  waiting for transfers between devices  18.9 us (15%)
  local copies, waits for them, and re-layouts  2.95 us (2%)
    pallas_call x35, Pallas kernels, call(): pl.pallas_call(body, out_shape=outs, in_specs=[whole(pltpu.SMEM)] * scala...  49.9 us
    ppermute x36, starting transfers between devices, swap(): lax.ppermute(value, BOTH, [(source, source ^ mask) for source in range(de...  47 us
    ppermute x36, waiting for transfers between devices, swap(): lax.ppermute(value, BOTH, [(source, source ^ mask) for source in range(de...  18.9 us
    pallas_call x1, Pallas kernels, per_device(): pl.pallas_call(functools.partial(setup_kernel, pairs), out_shape=[bf16(ha...  5.02 us
    ppermute x4, starting transfers between devices, halo(): lax.ppermute(other, BOTH, outward + [(target, source) for source, target...  3.01 us
    unnamed x13, local copies, waits for them, and re-layouts  2.95 us
  transfers between devices with their start and end apart: 40, of which 15 were waited for; matrix products, arithmetic and copies ran while one was open for 0% of the time, Pallas kernels for 20%

profile of v1, /device:TPU:0, one launch (start us, length us, event | category | flops | bytes accessed | tf_op | source)
XLA Modules:
  0.0 127.8 jit_solution(11750349264940711453)
XLA Ops:
  0.6 2.2 %copy.7 = f32[3,2048]{0,1:T(8,128)} copy(f32[3,2048]{1,0:T(4,128)} %lane_ref.2) | data formatting | bytes 49152 | tf_op args[1]
  3.6 5.0 %shard_map.68 = (bf16[2,512,512]{2,1,0:T(8,128)(2,1)S(1)}, bf16[2,512,512]{2,1,0:T(8,128)(2,1)S(1)}, bf16[896,2048]{1,0:T(8,128)(2,1)S(1)}, bf16[896,2048]{1,0:T(8,128)(2,1)S(1)}) custom-call(f32[3,2048]{1,0:T(4,128)S(1)} %copy-done.4, f32[2048,3]{1,0:T(8,128)} %bitcast.3, f32[7,128,2048]{2,1,0:T(8,128)} %basis_ref.1), custom_call_target="tpu_custom_call" | custom-call | flops 3000000000 | bytes 1048576 | tf_op jit(solution)/shard_map/pallas_call | solution.py:523
  8.6 2.3 %shard_map.70 = (f32[32,384]{1,0:T(8,128)S(1)}, f32[80,128]{1,0:T(8,128)S(1)}, f32[80,128]{1,0:T(8,128)S(1)}, f32[8,128]{1,0:T(8,128)S(1)}) custom-call(s32[1]{0:T(128)S(6)} %select_n.7.core_ref.refs_0_.refs_1_, f32[32,2048]{1,0:T(8,128)S(1)} %copy-done, bf16[896,2048]{1,0:T(8,128)(2,1)S(1)} %get-tuple-element.114.high_ref.refs_1_, ...), custom_call_target="tpu_custom_call" | custom-call | flops 3000000000 | bytes 1048576 | tf_op jit(solution)/shard_map/pallas_call | solution.py:82
  12.4 5.3 %collective-permute-start.5 = (f32[72,128]{1,0:T(8,128)S(1)}, f32[72,128]{1,0:T(8,128)S(1)}, u32[]{:S(2)}, u32[]{:S(2)}) collective-permute-start(f32[72,128]{1,0:T(8,128)S(1)} %get-tuple-element.121.refs_1_), channel_id=1, source_target_pairs={{0,6},{1,7},{2,4},{3,5},{4,2},{5,3},{6,0},{7,1},{8,14},{9,15},{10,... | collective-permute-start | bytes 110600 | tf_op jit(solution)/shard_map/ppermute | solution.py:458
  19.1 6.7 %shard_map.72 = (bf16[2,512,512]{2,1,0:T(8,128)(2,1)S(1)}, bf16[2,512,512]{2,1,0:T(8,128)(2,1)S(1)}, bf16[3,512,512]{2,1,0:T(8,128)(2,1)S(1)}, bf16[3,512,512]{2,1,0:T(8,128)(2,1)S(1)}) custom-call(f32[3,2048]{1,0:T(4,128)S(1)} %copy-done.5, f32[2048,3]{1,0:T(8,128)S(1)} %bitcast.4), custom_call_target="tpu_custom_call" | custom-call | flops 6000000000 | bytes 1048576 | tf_op jit(solution)/shard_map/pallas_call | solution.py:82
  25.9 5.1 %collective-permute-start.8 = (f32[40,128]{1,0:T(8,128)S(1)}, f32[40,128]{1,0:T(8,128)S(1)}, u32[]{:S(2)}, u32[]{:S(2)}) collective-permute-start(f32[40,128]{1,0:T(8,128)S(1)} %get-tuple-element.131.refs_1_), channel_id=1, source_target_pairs={{0,24},{1,25},{2,26},{3,27},{4,28},{5,29},{6,30},{7,31},{8,16},{9,... | collective-permute-start | bytes 61448 | tf_op jit(solution)/shard_map/ppermute | solution.py:458
  33.3 1.8 %shard_map.75.refs_7_ = f32[32,1024]{1,0:T(8,128)S(1)} custom-call(s32[1]{0:T(128)} %bitcast.place_ref.refs_0_, s32[4,3]{1,0:T(4,128)S(1)} %copy-done.3, f32[32,2048]{1,0:T(8,128)S(1)} %copy-done, f32[1,2048]{1,0:T(1,128)S(1)} %bitcast.7, bf16[2,512,512]{2,1,0:T(8,128)(2,1)S(1)} %get-tuple-element.139.high_ref, ...), custom_call_target="tpu_custom_call" | custom-call | flops 1500000000 | bytes 1048576 | tf_op jit(solution)/shard_map/pallas_call | solution.py:82
  35.2 2.7 %shard_map.74 = (bf16[2,512,512]{2,1,0:T(8,128)(2,1)S(1)}, bf16[2,512,512]{2,1,0:T(8,128)(2,1)S(1)}) custom-call(s32[1]{0:T(128)S(6)} %select_n.7.core_ref.refs_0_.refs_1_, f32[2048,3]{1,0:T(8,128)S(1)} %bitcast.5, f32[40,512]{1,0:T(8,128)S(1)} %collective-permute-done.refs_1_.refs_3_, f32[40,512]{1,0:T(8,128)S(1)} %collective-permute-done.1.refs_2_.refs_4_), custom_call_target="tpu_custom_call" | custom-call | flops 3000000000 | bytes 1048576 | tf_op jit(solution)/shard_map/pallas_call | solution.py:82
  42.9 2.9 %shard_map.82 = (f32[32,384]{1,0:T(8,128)S(1)}, f32[80,128]{1,0:T(8,128)S(1)}, f32[80,128]{1,0:T(8,128)S(1)}, f32[8,128]{1,0:T(8,128)}) custom-call(s32[1]{0:T(128)S(6)} %select_n.7.core_ref.refs_0_.refs_1_, f32[32,2048]{1,0:T(8,128)S(1)} %get-tuple-element.155.field_ref.refs_10_.refs_12_.refs_8_, bf16[896,2048]{1,0:T(8,128)(2,1)S(1)} %get-tuple-element.114.high_ref.refs_1_, ...), custom_call_target="tpu_custom_call" | custom-call | flops 3000000000 | bytes 1048576 | tf_op jit(solution)/shard_map/pallas_call | solution.py:82
  52.1 3.8 %collective-permute-start.15 = (f32[80,128]{1,0:T(8,128)S(1)}, f32[80,128]{1,0:T(8,128)S(1)}, u32[]{:S(2)}, u32[]{:S(2)}) collective-permute-start(f32[80,128]{1,0:T(8,128)S(1)} %get-tuple-element.161.refs_1_), channel_id=1, source_target_pairs={{0,6},{1,7},{2,4},{3,5},{4,2},{5,3},{6,0},{7,1},{8,14},{9,15},{10,... | collective-permute-start | bytes 122888 | tf_op jit(solution)/shard_map/ppermute | solution.py:458
  58.1 1.8 %collective-permute-done.14.refs_3_ = f32[80,128]{1,0:T(8,128)S(1)} collective-permute-done((f32[80,128]{1,0:T(8,128)S(1)}, f32[80,128]{1,0:T(8,128)S(1)}, u32[]{:S(2)}, u32[]{:S(2)}) %collective-permute-start.14) | collective-permute-done | bytes 40992 | tf_op jit(solution)/shard_map/ppermute | solution.py:458
  60.3 4.6 %collective-permute-start.18 = (f32[48,128]{1,0:T(8,128)S(1)}, f32[48,128]{1,0:T(8,128)S(1)}, u32[]{:S(2)}, u32[]{:S(2)}) collective-permute-start(f32[48,128]{1,0:T(8,128)S(1)} %get-tuple-element.163.refs_1_), channel_id=1, source_target_pairs={{0,24},{1,25},{2,26},{3,27},{4,28},{5,29},{6,30},{7,31},{8,16},{9,... | collective-permute-start | bytes 73736 | tf_op jit(solution)/shard_map/ppermute | solution.py:458
  66.7 2.9 %collective-permute-done.17.refs_3_ = f32[48,128]{1,0:T(8,128)S(1)} collective-permute-done((f32[48,128]{1,0:T(8,128)S(1)}, f32[48,128]{1,0:T(8,128)S(1)}, u32[]{:S(2)}, u32[]{:S(2)}) %collective-permute-start.17) | collective-permute-done | bytes 24608 | tf_op jit(solution)/shard_map/ppermute | solution.py:458
  73.0 2.3 %shard_map.88 = (f32[32,384]{1,0:T(8,128)S(1)}, f32[80,128]{1,0:T(8,128)S(1)}, f32[80,128]{1,0:T(8,128)S(1)}, f32[8,128]{1,0:T(8,128)S(1)}) custom-call(s32[1]{0:T(128)S(6)} %select_n.7.core_ref.refs_0_.refs_1_, f32[32,2048]{1,0:T(8,128)S(1)} %get-tuple-element.177.field_ref.refs_7_.refs_9_, bf16[896,2048]{1,0:T(8,128)(2,1)S(1)} %get-tuple-element.114.high_ref.refs_1_, ...), custom_call_target="tpu_custom_call" | custom-call | flops 3000000000 | bytes 1048576 | tf_op jit(solution)/shard_map/pallas_call | solution.py:82
  76.6 3.1 %collective-permute-start.23 = (f32[72,128]{1,0:T(8,128)S(1)}, f32[72,128]{1,0:T(8,128)S(1)}, u32[]{:S(2)}, u32[]{:S(2)}) collective-permute-start(f32[72,128]{1,0:T(8,128)S(1)} %get-tuple-element.176.refs_1_), channel_id=1, source_target_pairs={{0,6},{1,7},{2,4},{3,5},{4,2},{5,3},{6,0},{7,1},{8,14},{9,15},{10,... | collective-permute-start | bytes 110600 | tf_op jit(solution)/shard_map/ppermute | solution.py:458
  84.3 1.8 %shard_map.90.refs_7_ = f32[32,1024]{1,0:T(8,128)S(1)} custom-call(s32[1]{0:T(128)} %bitcast.place_ref.refs_0_, s32[4,3]{1,0:T(4,128)S(1)} %copy-done.3, f32[32,2048]{1,0:T(8,128)S(1)} %get-tuple-element.177.field_ref.refs_7_.refs_9_, f32[1,2048]{1,0:T(1,128)S(1)} %bitcast.11, bf16[2,512,512]{2,1,0:T(8,128)(2,1)S(1)} %get-tuple-element.139.high_ref, ...), custom_call_target="tpu_custom_call" | custom-call | flops 1500000000 | bytes 1048576 | tf_op jit(solution)/shard_map/pallas_call | solution.py:82
  86.2 3.3 %collective-permute-start.26 = (f32[40,128]{1,0:T(8,128)S(1)}, f32[40,128]{1,0:T(8,128)S(1)}, u32[]{:S(2)}, u32[]{:S(2)}) collective-permute-start(f32[40,128]{1,0:T(8,128)S(1)} %get-tuple-element.181.refs_1_), channel_id=1, source_target_pairs={{0,24},{1,25},{2,26},{3,27},{4,28},{5,29},{6,30},{7,31},{8,16},{9,... | collective-permute-start | bytes 61448 | tf_op jit(solution)/shard_map/ppermute | solution.py:458
  92.0 2.2 %collective-permute-done.25.refs_3_ = f32[40,128]{1,0:T(8,128)S(1)} collective-permute-done((f32[40,128]{1,0:T(8,128)S(1)}, f32[40,128]{1,0:T(8,128)S(1)}, u32[]{:S(2)}, u32[]{:S(2)}) %collective-permute-start.25) | collective-permute-done | bytes 20512 | tf_op jit(solution)/shard_map/ppermute | solution.py:458
  99.1 2.9 %shard_map.98 = (f32[32,384]{1,0:T(8,128)S(1)}, f32[80,128]{1,0:T(8,128)S(1)}, f32[80,128]{1,0:T(8,128)S(1)}, f32[8,128]{1,0:T(8,128)}) custom-call(s32[1]{0:T(128)S(6)} %select_n.7.core_ref.refs_0_.refs_1_, f32[32,2048]{1,0:T(8,128)S(1)} %get-tuple-element.206.field_ref.refs_10_, bf16[896,2048]{1,0:T(8,128)(2,1)S(1)} %get-tuple-element.114.high_ref.refs_1_, ...), custom_call_target="tpu_custom_call" | custom-call | flops 3000000000 | bytes 1048576 | tf_op jit(solution)/shard_map/pallas_call | solution.py:82
  103.1 1.8 %shard_map.96.refs_7_ = f32[32,1024]{1,0:T(8,128)S(1)} custom-call(s32[1]{0:T(128)} %bitcast.place_ref.refs_0_, s32[4,3]{1,0:T(4,128)S(1)} %copy-done.3, f32[32,2048]{1,0:T(8,128)S(1)} %get-tuple-element.206.field_ref.refs_10_, f32[1,2048]{1,0:T(1,128)S(1)} %bitcast.13, bf16[2,512,512]{2,1,0:T(8,128)(2,1)S(1)} %get-tuple-element.139.high_ref, ...), custom_call_target="tpu_custom_call" | custom-call | flops 1500000000 | bytes 1048576 | tf_op jit(solution)/shard_map/pallas_call | solution.py:82
  108.4 2.3 %collective-permute-start.35 = (f32[80,128]{1,0:T(8,128)S(1)}, f32[80,128]{1,0:T(8,128)S(1)}, u32[]{:S(2)}, u32[]{:S(2)}) collective-permute-start(f32[80,128]{1,0:T(8,128)S(1)} %get-tuple-element.216.refs_1_), channel_id=1, source_target_pairs={{0,6},{1,7},{2,4},{3,5},{4,2},{5,3},{6,0},{7,1},{8,14},{9,15},{10,... | collective-permute-start | bytes 122888 | tf_op jit(solution)/shard_map/ppermute | solution.py:458
  116.1 2.8 %collective-permute-start.38 = (f32[48,128]{1,0:T(8,128)S(1)}, f32[48,128]{1,0:T(8,128)S(1)}, u32[]{:S(2)}, u32[]{:S(2)}) collective-permute-start(f32[48,128]{1,0:T(8,128)S(1)} %get-tuple-element.218.refs_1_), channel_id=1, source_target_pairs={{0,24},{1,25},{2,26},{3,27},{4,28},{5,29},{6,30},{7,31},{8,16},{9,... | collective-permute-start | bytes 73736 | tf_op jit(solution)/shard_map/ppermute | solution.py:458
  121.8 1.9 %collective-permute-done.37.refs_3_ = f32[48,128]{1,0:T(8,128)S(1)} collective-permute-done((f32[48,128]{1,0:T(8,128)S(1)}, f32[48,128]{1,0:T(8,128)S(1)}, u32[]{:S(2)}, u32[]{:S(2)}) %collective-permute-start.37) | collective-permute-done | bytes 24608 | tf_op jit(solution)/shard_map/ppermute | solution.py:458
  125.6 2.2 %shard_map.103 = (f32[32,2048]{1,0:T(8,128)}, f32[32,2048]{1,0:T(8,128)}) custom-call(s32[1]{0:T(128)S(6)} %select_n.7.core_ref.refs_0_.refs_1_, bf16[896,2048]{1,0:T(8,128)(2,1)S(1)} %get-tuple-element.114.high_ref.refs_1_, bf16[896,2048]{1,0:T(8,128)(2,1)S(1)} %get-tuple-element.115.low_ref.refs_2_, f32[32,2048]{1,0:T(8,128)S(1)} %get-tuple-element.211.refs_3_, ...), custom_call_target="tpu_custom_call" | custom-call | flops 1500000000 | bytes 1048576 | tf_op jit(solution)/shard_map/pallas_call | solution.py:82
  (105 shorter events, 53.0 us)
Async XLA Ops:
  11.5 23.7 %collective-permute-start = (f32[40,512]{1,0:T(8,128)S(1)}, f32[40,512]{1,0:T(8,128)S(1)}, u32[]{:S(2)}, u32[]{:S(2)}) collective-permute-start(f32[40,512]{1,0:T(8,128)S(1)} %get-tuple-element.116), channel_id=1, source_target_pairs={{0,1},{1,0},{2,3},{3,2},{4,5},{5,4},{6,7},{7,6},{8,9},{9,8},{10,11... | collective-permute-start | bytes 245768 | tf_op jit(solution)/shard_map/ppermute | solution.py:458
  11.6 23.6 %collective-permute-start.1 = (f32[40,512]{1,0:T(8,128)S(1)}, f32[40,512]{1,0:T(8,128)S(1)}, u32[]{:S(2)}, u32[]{:S(2)}) collective-permute-start(f32[40,512]{1,0:T(8,128)S(1)} %get-tuple-element.117), channel_id=1, source_target_pairs={{1,2},{3,4},{5,6},{7,8},{9,10},{11,12},{13,14},{15,16},{17,18},{19... | collective-permute-start | bytes 245768 | tf_op jit(solution)/shard_map/ppermute | solution.py:463
  12.4 13.5 %collective-permute-start.5 = (f32[72,128]{1,0:T(8,128)S(1)}, f32[72,128]{1,0:T(8,128)S(1)}, u32[]{:S(2)}, u32[]{:S(2)}) collective-permute-start(f32[72,128]{1,0:T(8,128)S(1)} %get-tuple-element.121.refs_1_), channel_id=1, source_target_pairs={{0,6},{1,7},{2,4},{3,5},{4,2},{5,3},{6,0},{7,1},{8,14},{9,15},{10,... | collective-permute-start | bytes 110600 | tf_op jit(solution)/shard_map/ppermute | solution.py:458
  17.7 8.2 %collective-permute-start.4 = (f32[72,128]{1,0:T(8,128)S(1)}, f32[72,128]{1,0:T(8,128)S(1)}, u32[]{:S(2)}, u32[]{:S(2)}) collective-permute-start(f32[72,128]{1,0:T(8,128)S(1)} %get-tuple-element.121.refs_1_), channel_id=1, source_target_pairs={{0,4},{1,5},{2,6},{3,7},{4,0},{5,1},{6,2},{7,3},{8,12},{9,13},{10,... | collective-permute-start | bytes 110600 | tf_op jit(solution)/shard_map/ppermute | solution.py:458
  18.0 7.8 %collective-permute-start.3 = (f32[72,128]{1,0:T(8,128)S(1)}, f32[72,128]{1,0:T(8,128)S(1)}, u32[]{:S(2)}, u32[]{:S(2)}) collective-permute-start(f32[72,128]{1,0:T(8,128)S(1)} %get-tuple-element.121.refs_1_), channel_id=1, source_target_pairs={{0,2},{1,3},{2,0},{3,1},{4,6},{5,7},{6,4},{7,5},{8,10},{9,11},{10,... | collective-permute-start | bytes 110600 | tf_op jit(solution)/shard_map/ppermute | solution.py:458
  25.9 12.0 %collective-permute-start.8 = (f32[40,128]{1,0:T(8,128)S(1)}, f32[40,128]{1,0:T(8,128)S(1)}, u32[]{:S(2)}, u32[]{:S(2)}) collective-permute-start(f32[40,128]{1,0:T(8,128)S(1)} %get-tuple-element.131.refs_1_), channel_id=1, source_target_pairs={{0,24},{1,25},{2,26},{3,27},{4,28},{5,29},{6,30},{7,31},{8,16},{9,... | collective-permute-start | bytes 61448 | tf_op jit(solution)/shard_map/ppermute | solution.py:458
  30.9 6.9 %collective-permute-start.7 = (f32[40,128]{1,0:T(8,128)S(1)}, f32[40,128]{1,0:T(8,128)S(1)}, u32[]{:S(2)}, u32[]{:S(2)}) collective-permute-start(f32[40,128]{1,0:T(8,128)S(1)} %get-tuple-element.131.refs_1_), channel_id=1, source_target_pairs={{0,16},{1,17},{2,18},{3,19},{4,20},{5,21},{6,22},{7,23},{8,24},{9,... | collective-permute-start | bytes 61448 | tf_op jit(solution)/shard_map/ppermute | solution.py:458
  30.9 6.9 %collective-permute-start.6 = (f32[40,128]{1,0:T(8,128)S(1)}, f32[40,128]{1,0:T(8,128)S(1)}, u32[]{:S(2)}, u32[]{:S(2)}) collective-permute-start(f32[40,128]{1,0:T(8,128)S(1)} %get-tuple-element.131.refs_1_), channel_id=1, source_target_pairs={{0,8},{1,9},{2,10},{3,11},{4,12},{5,13},{6,14},{7,15},{8,0},{9,1},... | collective-permute-start | bytes 61448 | tf_op jit(solution)/shard_map/ppermute | solution.py:458
  52.1 5.9 %collective-permute-start.15 = (f32[80,128]{1,0:T(8,128)S(1)}, f32[80,128]{1,0:T(8,128)S(1)}, u32[]{:S(2)}, u32[]{:S(2)}) collective-permute-start(f32[80,128]{1,0:T(8,128)S(1)} %get-tuple-element.161.refs_1_), channel_id=1, source_target_pairs={{0,6},{1,7},{2,4},{3,5},{4,2},{5,3},{6,0},{7,1},{8,14},{9,15},{10,... | collective-permute-start | bytes 122888 | tf_op jit(solution)/shard_map/ppermute | solution.py:458
  60.3 6.4 %collective-permute-start.18 = (f32[48,128]{1,0:T(8,128)S(1)}, f32[48,128]{1,0:T(8,128)S(1)}, u32[]{:S(2)}, u32[]{:S(2)}) collective-permute-start(f32[48,128]{1,0:T(8,128)S(1)} %get-tuple-element.163.refs_1_), channel_id=1, source_target_pairs={{0,24},{1,25},{2,26},{3,27},{4,28},{5,29},{6,30},{7,31},{8,16},{9,... | collective-permute-start | bytes 73736 | tf_op jit(solution)/shard_map/ppermute | solution.py:458
  64.9 4.7 %collective-permute-start.17 = (f32[48,128]{1,0:T(8,128)S(1)}, f32[48,128]{1,0:T(8,128)S(1)}, u32[]{:S(2)}, u32[]{:S(2)}) collective-permute-start(f32[48,128]{1,0:T(8,128)S(1)} %get-tuple-element.163.refs_1_), channel_id=1, source_target_pairs={{0,16},{1,17},{2,18},{3,19},{4,20},{5,21},{6,22},{7,23},{8,24},{9,... | collective-permute-start | bytes 73736 | tf_op jit(solution)/shard_map/ppermute | solution.py:458
  64.9 4.7 %collective-permute-start.16 = (f32[48,128]{1,0:T(8,128)S(1)}, f32[48,128]{1,0:T(8,128)S(1)}, u32[]{:S(2)}, u32[]{:S(2)}) collective-permute-start(f32[48,128]{1,0:T(8,128)S(1)} %get-tuple-element.163.refs_1_), channel_id=1, source_target_pairs={{0,8},{1,9},{2,10},{3,11},{4,12},{5,13},{6,14},{7,15},{8,0},{9,1},... | collective-permute-start | bytes 73736 | tf_op jit(solution)/shard_map/ppermute | solution.py:458
  75.5 15.1 %collective-permute-start.27 = (f32[32,512]{1,0:T(8,128)S(1)}, f32[32,512]{1,0:T(8,128)S(1)}, u32[]{:S(2)}, u32[]{:S(2)}) collective-permute-start(f32[32,512]{1,0:T(8,128)S(1)} %get-tuple-element.182), channel_id=1, source_target_pairs={{0,1},{1,0},{2,3},{3,2},{4,5},{5,4},{6,7},{7,6},{8,9},{9,8},{10,11... | collective-permute-start | bytes 196616 | tf_op jit(solution)/shard_map/ppermute | solution.py:458
  75.9 14.8 %collective-permute-start.28 = (f32[32,512]{1,0:T(8,128)S(1)}, f32[32,512]{1,0:T(8,128)S(1)}, u32[]{:S(2)}, u32[]{:S(2)}) collective-permute-start(f32[32,512]{1,0:T(8,128)S(1)} %get-tuple-element.183), channel_id=1, source_target_pairs={{1,2},{3,4},{5,6},{7,8},{9,10},{11,12},{13,14},{15,16},{17,18},{19... | collective-permute-start | bytes 196616 | tf_op jit(solution)/shard_map/ppermute | solution.py:463
  76.6 9.5 %collective-permute-start.23 = (f32[72,128]{1,0:T(8,128)S(1)}, f32[72,128]{1,0:T(8,128)S(1)}, u32[]{:S(2)}, u32[]{:S(2)}) collective-permute-start(f32[72,128]{1,0:T(8,128)S(1)} %get-tuple-element.176.refs_1_), channel_id=1, source_target_pairs={{0,6},{1,7},{2,4},{3,5},{4,2},{5,3},{6,0},{7,1},{8,14},{9,15},{10,... | collective-permute-start | bytes 110600 | tf_op jit(solution)/shard_map/ppermute | solution.py:458
  79.7 6.4 %collective-permute-start.22 = (f32[72,128]{1,0:T(8,128)S(1)}, f32[72,128]{1,0:T(8,128)S(1)}, u32[]{:S(2)}, u32[]{:S(2)}) collective-permute-start(f32[72,128]{1,0:T(8,128)S(1)} %get-tuple-element.176.refs_1_), channel_id=1, source_target_pairs={{0,4},{1,5},{2,6},{3,7},{4,0},{5,1},{6,2},{7,3},{8,12},{9,13},{10,... | collective-permute-start | bytes 110600 | tf_op jit(solution)/shard_map/ppermute | solution.py:458
  81.4 4.8 %collective-permute-start.21 = (f32[72,128]{1,0:T(8,128)S(1)}, f32[72,128]{1,0:T(8,128)S(1)}, u32[]{:S(2)}, u32[]{:S(2)}) collective-permute-start(f32[72,128]{1,0:T(8,128)S(1)} %get-tuple-element.176.refs_1_), channel_id=1, source_target_pairs={{0,2},{1,3},{2,0},{3,1},{4,6},{5,7},{6,4},{7,5},{8,10},{9,11},{10,... | collective-permute-start | bytes 110600 | tf_op jit(solution)/shard_map/ppermute | solution.py:458
  86.2 5.8 %collective-permute-start.26 = (f32[40,128]{1,0:T(8,128)S(1)}, f32[40,128]{1,0:T(8,128)S(1)}, u32[]{:S(2)}, u32[]{:S(2)}) collective-permute-start(f32[40,128]{1,0:T(8,128)S(1)} %get-tuple-element.181.refs_1_), channel_id=1, source_target_pairs={{0,24},{1,25},{2,26},{3,27},{4,28},{5,29},{6,30},{7,31},{8,16},{9,... | collective-permute-start | bytes 61448 | tf_op jit(solution)/shard_map/ppermute | solution.py:458
  89.5 4.7 %collective-permute-start.25 = (f32[40,128]{1,0:T(8,128)S(1)}, f32[40,128]{1,0:T(8,128)S(1)}, u32[]{:S(2)}, u32[]{:S(2)}) collective-permute-start(f32[40,128]{1,0:T(8,128)S(1)} %get-tuple-element.181.refs_1_), channel_id=1, source_target_pairs={{0,16},{1,17},{2,18},{3,19},{4,20},{5,21},{6,22},{7,23},{8,24},{9,... | collective-permute-start | bytes 61448 | tf_op jit(solution)/shard_map/ppermute | solution.py:458
  89.5 4.7 %collective-permute-start.24 = (f32[40,128]{1,0:T(8,128)S(1)}, f32[40,128]{1,0:T(8,128)S(1)}, u32[]{:S(2)}, u32[]{:S(2)}) collective-permute-start(f32[40,128]{1,0:T(8,128)S(1)} %get-tuple-element.181.refs_1_), channel_id=1, source_target_pairs={{0,8},{1,9},{2,10},{3,11},{4,12},{5,13},{6,14},{7,15},{8,0},{9,1},... | collective-permute-start | bytes 61448 | tf_op jit(solution)/shard_map/ppermute | solution.py:458
  102.0 4.7 %collective-permute-start.30 = (f32[32,512]{1,0:T(8,128)S(1)}, f32[32,512]{1,0:T(8,128)S(1)}, u32[]{:S(2)}, u32[]{:S(2)}) collective-permute-start(f32[32,512]{1,0:T(8,128)S(1)} %get-tuple-element.204), channel_id=1, source_target_pairs={{0,1},{1,0},{2,3},{3,2},{4,5},{5,4},{6,7},{7,6},{8,9},{9,8},{10,11... | collective-permute-start | bytes 196616 | tf_op jit(solution)/shard_map/ppermute | solution.py:458
  108.4 4.9 %collective-permute-start.35 = (f32[80,128]{1,0:T(8,128)S(1)}, f32[80,128]{1,0:T(8,128)S(1)}, u32[]{:S(2)}, u32[]{:S(2)}) collective-permute-start(f32[80,128]{1,0:T(8,128)S(1)} %get-tuple-element.216.refs_1_), channel_id=1, source_target_pairs={{0,6},{1,7},{2,4},{3,5},{4,2},{5,3},{6,0},{7,1},{8,14},{9,15},{10,... | collective-permute-start | bytes 122888 | tf_op jit(solution)/shard_map/ppermute | solution.py:458
  116.1 5.7 %collective-permute-start.38 = (f32[48,128]{1,0:T(8,128)S(1)}, f32[48,128]{1,0:T(8,128)S(1)}, u32[]{:S(2)}, u32[]{:S(2)}) collective-permute-start(f32[48,128]{1,0:T(8,128)S(1)} %get-tuple-element.218.refs_1_), channel_id=1, source_target_pairs={{0,24},{1,25},{2,26},{3,27},{4,28},{5,29},{6,30},{7,31},{8,16},{9,... | collective-permute-start | bytes 73736 | tf_op jit(solution)/shard_map/ppermute | solution.py:458
  119.0 4.7 %collective-permute-start.37 = (f32[48,128]{1,0:T(8,128)S(1)}, f32[48,128]{1,0:T(8,128)S(1)}, u32[]{:S(2)}, u32[]{:S(2)}) collective-permute-start(f32[48,128]{1,0:T(8,128)S(1)} %get-tuple-element.218.refs_1_), channel_id=1, source_target_pairs={{0,16},{1,17},{2,18},{3,19},{4,20},{5,21},{6,22},{7,23},{8,24},{9,... | collective-permute-start | bytes 73736 | tf_op jit(solution)/shard_map/ppermute | solution.py:458
  (22 other events, 113.1 us)
